TPU v7x, 256 devices: a whole 4x4x8 slice. The times are simulated.
256 devices in a mesh: seq: 16 (over y, z_hi), pool: 2 (over z_lo), dp: 8 (over x, core).
Axes of the slice: x: 4, y: 4, z: 8 (z_hi: 4, z_lo: 2; z = z_hi * 2 + z_lo), core: 2. Of those that a mesh axis runs over, the one named last changes fastest.
Arguments:
- queries: bfloat16 [8, 2, 2048, 4096], P('dp', 'pool', 'seq'), may hold values from -160 to 160
- keys: bfloat16 [8, 2, 2048, 512], P('dp', 'pool', 'seq'), may hold values from -5 to 5
- values: bfloat16 [8, 2, 2048, 512], P('dp', 'pool', 'seq'), may hold values from -6 to 6
- old_keys: bfloat16 [8, 2, 512, 512], P('dp', 'pool', 'seq'), may hold values from -6 to 6
- old_values: bfloat16 [8, 2, 512, 512], P('dp', 'pool', 'seq'), may hold values from -6 to 6
- out_grad: bfloat16 [8, 2, 2048, 4096], P('dp', 'pool', 'seq'), may hold values from -6 to 6
- inputs: bfloat16 [8, 2, 2048, 8192], P('dp', 'pool', 'seq'), may hold values from -6 to 6
- reads: int32 [8, 2, 2, 4], P('dp', 'pool'), may hold values 0 or 1
Outputs:
- query_grad: bfloat16 [8, 2, 2048, 4096], P('dp', 'pool', 'seq')
- key_grad: bfloat16 [8, 2, 2048, 512], P('dp', 'pool', 'seq')
- value_grad: bfloat16 [8, 2, 2048, 512], P('dp', 'pool', 'seq')
- old_key_grad: bfloat16 [8, 2, 512, 512], P('dp', 'pool', 'seq')
- old_value_grad: bfloat16 [8, 2, 512, 512], P('dp', 'pool', 'seq')
- weight_grad: bfloat16 [8192, 512], P(('seq', 'pool'))
All inputs are finite; a program needn't handle non-finite values. No bound on the sum of `reads` on one device may be relied on, other than what follows from the above.
Results may differ from a plain program's by a relative error of at most 0.025.
Values may be sent and summed in bfloat16 or wider, within the bound.
A program may use at most 128 MiB of HBM per device.

v0:
```python
import math

import jax
import jax.numpy as jnp
from jax import lax
from jax.sharding import PartitionSpec as P

HD = 128
QCHUNKS = 2
OLD_STRETCHES = 4


NEG = -1e30


def swapped(block, axis, distance):
    count = lax.axis_size(axis)
    route = []
    for low in range(count):
        high = low | 1 << distance
        if high != low and high < count:
            route += [(low, high), (high, low)]
    return lax.ppermute(block, axis, route)


def widen(block, copies):
    count = block.shape[0]
    heads = block.shape[1] // HD
    spread = jnp.broadcast_to(block.reshape(count, heads, 1, HD), (count, heads, copies, HD))
    return spread.reshape(count, heads * copies * HD)


def narrow(block, copies):
    count = block.shape[0]
    heads = block.shape[1] // (HD * copies)
    return jnp.sum(block.reshape(count, heads, copies, HD).astype(jnp.float32), axis=2).reshape(
        count, heads * HD
    )


def on_device(queries, keys, values, old_keys, old_values, out_grad, inputs, reads):
    seq_count = lax.axis_size("seq")
    group_count = seq_count * lax.axis_size("pool")
    kv_heads = keys.shape[3] // HD
    copies = seq_count // kv_heads
    q_heads, g_heads = (
        lax.all_to_all(queries[0, 0], "seq", split_axis=1, concat_axis=0, tiled=True),
        lax.all_to_all(out_grad[0, 0], "seq", split_axis=1, concat_axis=0, tiled=True),
    )
    held_k, held_v = swapped((old_keys[0, 0], old_values[0, 0]), "pool", 0)
    cur_k, cur_v, past_k, past_v = (
        lax.all_to_all(widen(keys[0, 0], copies), "seq", split_axis=1, concat_axis=0, tiled=True),
        lax.all_to_all(widen(values[0, 0], copies), "seq", split_axis=1, concat_axis=0, tiled=True),
        lax.all_to_all(widen(held_k, copies), "seq", split_axis=1, concat_axis=0, tiled=True),
        lax.all_to_all(widen(held_v, copies), "seq", split_axis=1, concat_axis=0, tiled=True),
    )
    cur = q_heads.shape[0]
    past = past_k.shape[0]
    heads = q_heads.shape[1] // HD
    total = past + cur
    all_k = jnp.concatenate([past_k, cur_k], 0)
    all_v = jnp.concatenate([past_v, cur_v], 0)
    scale = HD ** (-0.5)
    block = math.gcd(cur, 512)
    count = cur // block
    span = cur // QCHUNKS
    width = past // OLD_STRETCHES
    stretch_map = (jnp.arange(past)[None, :] // width == jnp.arange(OLD_STRETCHES)[:, None]).astype(
        jnp.float32
    )
    read_map = jnp.dot(
        reads[0, 0].astype(jnp.float32), stretch_map, preferred_element_type=jnp.float32
    )
    q_blocks = q_heads.reshape(count, block, heads, HD)
    g_blocks = g_heads.reshape(count, block, heads, HD)
    key_cols = jnp.arange(cur)

    def step(carry, item):
        grad_k, grad_v = carry
        index, q_part, g_part = item
        rows = index * block + jnp.arange(block)
        which = (rows // span)[:, None] == jnp.arange(QCHUNKS)[None, :]
        old_ok = (
            jnp.dot(which.astype(jnp.float32), read_map, preferred_element_type=jnp.float32) > 0.5
        )
        new_ok = key_cols[None, :] <= rows[:, None]
        allowed = jnp.concatenate([old_ok, new_ok], 1)
        scores = (
            jnp.einsum("qhd,kd->hqk", q_part, all_k, preferred_element_type=jnp.float32) * scale
        )
        scores = jnp.where(allowed[None], scores, NEG)
        top = jnp.max(scores, -1, keepdims=True)
        expo = jnp.exp(scores - top)
        probs = expo / jnp.sum(expo, -1, keepdims=True)
        dprobs = jnp.einsum("qhd,kd->hqk", g_part, all_v, preferred_element_type=jnp.float32)
        delta = jnp.sum(probs * dprobs, -1, keepdims=True)
        dscores = (probs * (dprobs - delta)).astype(jnp.bfloat16)
        probs_low = probs.astype(jnp.bfloat16)
        grad_q = (
            jnp.einsum("hqk,kd->qhd", dscores, all_k, preferred_element_type=jnp.float32) * scale
        ).astype(jnp.bfloat16)
        term_k = (
            jnp.einsum("hqk,qhd->kd", dscores, q_part, preferred_element_type=jnp.float32) * scale
        )
        term_v = jnp.einsum("hqk,qhd->kd", probs_low, g_part, preferred_element_type=jnp.float32)
        return ((grad_k + term_k, grad_v + term_v), grad_q.reshape(block, heads * HD))

    start = (jnp.zeros((total, HD), jnp.float32), jnp.zeros((total, HD), jnp.float32))
    (grad_k, grad_v), q_grads = lax.scan(step, start, (jnp.arange(count), q_blocks, g_blocks))
    q_tokens = lax.all_to_all(
        q_grads.reshape(cur, heads * HD), "seq", split_axis=0, concat_axis=1, tiled=True
    )
    part_k = grad_k.astype(jnp.bfloat16)
    part_v = grad_v.astype(jnp.bfloat16)
    back = (
        lax.all_to_all(part_k[past:], "seq", split_axis=0, concat_axis=1, tiled=True),
        lax.all_to_all(part_v[past:], "seq", split_axis=0, concat_axis=1, tiled=True),
        lax.all_to_all(part_k[:past], "seq", split_axis=0, concat_axis=1, tiled=True),
        lax.all_to_all(part_v[:past], "seq", split_axis=0, concat_axis=1, tiled=True),
    )
    new_k, new_v, earlier_k, earlier_v = [narrow(piece, copies) for piece in back]
    key_grad = new_k.astype(jnp.bfloat16)
    value_grad = new_v.astype(jnp.bfloat16)
    return_k, return_v = swapped(
        (earlier_k.astype(jnp.bfloat16), earlier_v.astype(jnp.bfloat16)), "pool", 0
    )
    tokens_in = inputs[0, 0]
    shard = lax.psum_scatter(
        lax.dot_general(
            tokens_in, value_grad, (((0,), (0,)), ((), ())), preferred_element_type=jnp.float32
        ).astype(jnp.bfloat16),
        ("seq", "pool"),
        scatter_dimension=0,
        tiled=True,
    )
    ranks = group_count * lax.axis_size("dp")
    weight_grad = (lax.psum(shard, "dp").astype(jnp.float32) / ranks).astype(jnp.bfloat16)
    return (
        q_tokens[None, None],
        key_grad[None, None],
        value_grad[None, None],
        return_k[None, None],
        return_v[None, None],
        weight_grad,
    )


def solution(mesh):
    in_specs = (
        P("dp", "pool", "seq", None),
        P("dp", "pool", "seq", None),
        P("dp", "pool", "seq", None),
        P("dp", "pool", "seq", None),
        P("dp", "pool", "seq", None),
        P("dp", "pool", "seq", None),
        P("dp", "pool", "seq", None),
        P("dp", "pool", None, None),
    )
    out_specs = (
        P("dp", "pool", "seq", None),
        P("dp", "pool", "seq", None),
        P("dp", "pool", "seq", None),
        P("dp", "pool", "seq", None),
        P("dp", "pool", "seq", None),
        P(("seq", "pool"), None),
    )
    return jax.shard_map(
        on_device, mesh=mesh, in_specs=in_specs, out_specs=out_specs, check_vma=False
    )
```

profile of v0, /device:TPU:1, one launch (start us, length us, event | category | flops | bytes accessed | tf_op | source)
XLA Modules:
  0.0 655.9 jit_solution(15647848479177877529)
XLA Ops:
  7.2 2.6 collective-permute-start.1
  11.9 10.7 %all-to-all-start.4 = ((bf16[32,16,128]{2,0,1:T(8,128)(2,1)}), bf16[32,16,128]{2,0,1:T(8,128)(2,1)S(1)}, u32[]{:S(2)}, u32[]{:S(2)}) async-start(bf16[32,16,128]{2,0,1:T(8,128)(2,1)} %bitcast.13), calls=%async_computation.4 | async-start | bytes 262144 | tf_op jit(solution)/shard_map/all_to_all | solution.py:55
  22.7 9.6 %all-to-all-done.4 = bf16[32,16,128]{2,0,1:T(8,128)(2,1)S(1)} async-done(((bf16[32,16,128]{2,0,1:T(8,128)(2,1)}), bf16[32,16,128]{2,0,1:T(8,128)(2,1)S(1)}, u32[]{:S(2)}, u32[]{:S(2)}) %all-to-all-start.4) | async-done | bytes 131104 | tf_op jit(solution)/shard_map/all_to_all | solution.py:55
  33.0 3.5 all-to-all-start.1
  37.5 8.6 %all-to-all-done.1 = bf16[32,16,128]{2,0,1:T(8,128)(2,1)S(1)} async-done(((bf16[32,16,128]{2,0,1:T(8,128)(2,1)}), bf16[32,16,128]{2,0,1:T(8,128)(2,1)S(1)}, u32[]{:S(2)}, u32[]{:S(2)}) %all-to-all-start.1) | async-done | bytes 131104 | tf_op jit(solution)/shard_map/all_to_all | solution.py:54
  46.9 3.6 all-to-all-start.5
  51.6 12.5 %all-to-all-done.5 = bf16[128,16,128]{2,0,1:T(8,128)(2,1)S(1)} async-done(((bf16[128,16,128]{2,0,1:T(8,128)(2,1)}), bf16[128,16,128]{2,0,1:T(8,128)(2,1)S(1)}, u32[]{:S(2)}, u32[]{:S(2)}) %all-to-all-start.5) | async-done | bytes 524320 | tf_op jit(solution)/shard_map/all_to_all | solution.py:53
  65.0 4.3 all-to-all-start.2
  72.2 9.9 %all-to-all-done.2 = bf16[128,16,128]{0,2,1:T(8,128)(2,1)S(1)} async-done(((bf16[128,16,128]{0,2,1:T(8,128)(2,1)}), bf16[128,16,128]{0,2,1:T(8,128)(2,1)S(1)}, u32[]{:S(2)}, u32[]{:S(2)}) %all-to-all-start.2) | async-done | bytes 524320 | tf_op jit(solution)/shard_map/all_to_all | solution.py:52
  82.9 5.2 all-to-all-start
  91.0 16.3 %all-to-all-done = bf16[128,16,256]{2,0,1:T(8,128)(2,1)S(1)} async-done(((bf16[128,16,256]{2,0,1:T(8,128)(2,1)}), bf16[128,16,256]{2,0,1:T(8,128)(2,1)S(1)}, u32[]{:S(2)}, u32[]{:S(2)}) %all-to-all-start) | async-done | bytes 1048608 | tf_op jit(solution)/shard_map/all_to_all | solution.py:47
  107.3 5.6 all-to-all-start.3
  113.1 2.0 copy.79
  115.2 2.0 pad_maximum_fusion
  117.1 2.2 copy.84
  121.2 2.1 reshape.191
  123.4 6.7 %all-to-all-done.3 = bf16[128,16,256]{2,0,1:T(8,128)(2,1)} async-done(((bf16[128,16,256]{2,0,1:T(8,128)(2,1)}), bf16[128,16,256]{2,0,1:T(8,128)(2,1)}, u32[]{:S(2)}, u32[]{:S(2)}) %all-to-all-start.3) | async-done | bytes 1048608 | tf_op jit(solution)/shard_map/all_to_all | solution.py:48
  130.1 2.1 reshape.192
  132.2 155.3 %while.17 = (s32[]{:T(128)}, f32[2560,128]{1,0:T(8,128)S(1)}, f32[2560,128]{1,0:T(8,128)}, bf16[4,512,256]{2,1,0:T(8,128)(2,1)}, s32[4]{0:T(128)S(1)}, /*index=5...) while((s32[]{:T(128)}, f32[2560,128]{1,0:T(8,128)S(1)}, ...), condition=%wide.region_4.5_spmd.clone, body=%wide.region_0.4_spmd.clone.sunk | while | flops 3395103232 | bytes 144345392 | solution.py:109
  134.6 2.0 copy.145
  136.6 2.2 constant_dynamic-slice_fusion.3
  139.5 2.2 pad_add_fusion.2
  141.6 9.6 %fusion.79 = (f32[2,512]{1,0:T(2,128)S(1)}, f32[2,512,2560]{2,1,0:T(8,128)}) fusion(pred[512,2560]{1,0:T(8,128)(4,1)} %pad_add_fusion.2, bf16[2560,128]{0,1:T(8,128)(2,1)} %get-tuple-element.392, bf16[1,512,2,128]{3,2,1,0:T(2,128)(2,1)} %get-tuple-element.353), kind=kOutput, calls=%fused_computation.78.clone.1 | convolution fusion | flops 681576960 | bytes 12718080 | tf_op jit(solution)/shard_map/while/body/eval_jaxpr/sub | solution.py:93
  151.2 7.0 %fusion.83 = f32[2560,128]{1,0:T(8,128)} fusion(f32[2560,128]{1,0:T(8,128)} %get-tuple-element.374, pred[]{:T(512)S(6)} %compare.20, bf16[1,512,2,128]{3,2,1,0:T(2,128)(2,1)} %get-tuple-element.356, f32[2,512,2560]{2,1,0:T(8,128)} %get-tuple-element.354, f32[2,512]{1,0:T(2,128)S(1)} %get-tuple-element.355), kind=kOutput, calls=%fused_computation.24.clone.1 | convolution fusion | flops 676986880 | bytes 13373441 | tf_op jit(solution)/shard_map/while/body/eval_jaxpr/hqk,qhd->kd/dot_general | solution.py:105
  158.9 2.0 fusion.80
  162.6 2.5 fusion.84
  165.2 2.2 fusion.82
  173.2 2.0 copy.145
  175.2 2.2 constant_dynamic-slice_fusion.3
  178.0 2.2 pad_add_fusion.2
  180.2 9.6 %fusion.79 = (f32[2,512]{1,0:T(2,128)S(1)}, f32[2,512,2560]{2,1,0:T(8,128)}) fusion(pred[512,2560]{1,0:T(8,128)(4,1)} %pad_add_fusion.2, bf16[2560,128]{0,1:T(8,128)(2,1)} %get-tuple-element.392, bf16[1,512,2,128]{3,2,1,0:T(2,128)(2,1)} %get-tuple-element.353), kind=kOutput, calls=%fused_computation.78.clone.1 | convolution fusion | flops 681576960 | bytes 12718080 | tf_op jit(solution)/shard_map/while/body/eval_jaxpr/sub | solution.py:93
  189.7 7.4 %fusion.83 = f32[2560,128]{1,0:T(8,128)} fusion(f32[2560,128]{1,0:T(8,128)} %get-tuple-element.374, pred[]{:T(512)S(6)} %compare.20, bf16[1,512,2,128]{3,2,1,0:T(2,128)(2,1)} %get-tuple-element.356, f32[2,512,2560]{2,1,0:T(8,128)} %get-tuple-element.354, f32[2,512]{1,0:T(2,128)S(1)} %get-tuple-element.355), kind=kOutput, calls=%fused_computation.24.clone.1 | convolution fusion | flops 676986880 | bytes 13373441 | tf_op jit(solution)/shard_map/while/body/eval_jaxpr/hqk,qhd->kd/dot_general | solution.py:105
  197.8 2.0 fusion.80
  201.6 2.5 fusion.84
  204.1 2.2 fusion.82
  212.1 2.0 copy.145
  214.1 2.2 constant_dynamic-slice_fusion.3
  216.9 2.2 pad_add_fusion.2
  219.1 9.6 %fusion.79 = (f32[2,512]{1,0:T(2,128)S(1)}, f32[2,512,2560]{2,1,0:T(8,128)}) fusion(pred[512,2560]{1,0:T(8,128)(4,1)} %pad_add_fusion.2, bf16[2560,128]{0,1:T(8,128)(2,1)} %get-tuple-element.392, bf16[1,512,2,128]{3,2,1,0:T(2,128)(2,1)} %get-tuple-element.353), kind=kOutput, calls=%fused_computation.78.clone.1 | convolution fusion | flops 681576960 | bytes 12718080 | tf_op jit(solution)/shard_map/while/body/eval_jaxpr/sub | solution.py:93
  228.7 7.4 %fusion.83 = f32[2560,128]{1,0:T(8,128)} fusion(f32[2560,128]{1,0:T(8,128)} %get-tuple-element.374, pred[]{:T(512)S(6)} %compare.20, bf16[1,512,2,128]{3,2,1,0:T(2,128)(2,1)} %get-tuple-element.356, f32[2,512,2560]{2,1,0:T(8,128)} %get-tuple-element.354, f32[2,512]{1,0:T(2,128)S(1)} %get-tuple-element.355), kind=kOutput, calls=%fused_computation.24.clone.1 | convolution fusion | flops 676986880 | bytes 13373441 | tf_op jit(solution)/shard_map/while/body/eval_jaxpr/hqk,qhd->kd/dot_general | solution.py:105
  236.7 2.0 fusion.80
  240.5 2.5 fusion.84
  243.0 2.2 fusion.82
  251.0 2.0 copy.145
  253.0 2.2 constant_dynamic-slice_fusion.3
  255.8 2.2 pad_add_fusion.2
  258.0 9.6 %fusion.79 = (f32[2,512]{1,0:T(2,128)S(1)}, f32[2,512,2560]{2,1,0:T(8,128)}) fusion(pred[512,2560]{1,0:T(8,128)(4,1)} %pad_add_fusion.2, bf16[2560,128]{0,1:T(8,128)(2,1)} %get-tuple-element.392, bf16[1,512,2,128]{3,2,1,0:T(2,128)(2,1)} %get-tuple-element.353), kind=kOutput, calls=%fused_computation.78.clone.1 | convolution fusion | flops 681576960 | bytes 12718080 | tf_op jit(solution)/shard_map/while/body/eval_jaxpr/sub | solution.py:93
  267.6 7.4 %fusion.83 = f32[2560,128]{1,0:T(8,128)} fusion(f32[2560,128]{1,0:T(8,128)} %get-tuple-element.374, pred[]{:T(512)S(6)} %compare.20, bf16[1,512,2,128]{3,2,1,0:T(2,128)(2,1)} %get-tuple-element.356, f32[2,512,2560]{2,1,0:T(8,128)} %get-tuple-element.354, f32[2,512]{1,0:T(2,128)S(1)} %get-tuple-element.355), kind=kOutput, calls=%fused_computation.24.clone.1 | convolution fusion | flops 676986880 | bytes 13373441 | tf_op jit(solution)/shard_map/while/body/eval_jaxpr/hqk,qhd->kd/dot_general | solution.py:105
  275.6 2.0 fusion.80
  279.4 2.5 fusion.84
  281.9 2.2 fusion.82
  289.9 15.0 %all_to_all.176 = bf16[16,128,128]{2,1,0:T(8,128)(2,1)S(1)} all-to-all(bf16[16,128,128]{2,1,0:T(8,128)(2,1)S(1)} %bitcast.208), channel_id=1, replica_groups=mesh['seq'=16,'pool'=2,'dp'=8] {'seq'}, dimensions={0} | all-to-all | bytes 1048576 | tf_op jit(solution)/shard_map/all_to_all | solution.py:117
  306.7 5.6 fusion.42
  313.9 3.5 all-to-all-start.9
  319.0 8.0 %all-to-all-done.9 = bf16[16,32,128]{2,1,0:T(8,128)(2,1)S(1)} async-done(((bf16[16,32,128]{2,1,0:T(8,128)(2,1)}), bf16[16,32,128]{2,1,0:T(8,128)(2,1)S(1)}, u32[]{:S(2)}, u32[]{:S(2)}) %all-to-all-start.9) | async-done | bytes 131104 | tf_op jit(solution)/shard_map/all_to_all | solution.py:118
  326.9 6.2 all-to-all-start.10
  334.3 8.4 %all-to-all-done.10 = bf16[16,32,128]{2,1,0:T(8,128)(2,1)S(1)} async-done(((bf16[16,32,128]{2,1,0:T(8,128)(2,1)}), bf16[16,32,128]{2,1,0:T(8,128)(2,1)S(1)}, u32[]{:S(2)}, u32[]{:S(2)}) %all-to-all-start.10) | async-done | bytes 131104 | tf_op jit(solution)/shard_map/all_to_all | solution.py:119
  342.7 18.4 %all_to_all.177 = bf16[16,128,128]{2,1,0:T(8,128)(2,1)} all-to-all(bf16[16,128,128]{2,1,0:T(8,128)(2,1)S(1)} %bitcast.206), channel_id=1, replica_groups=mesh['seq'=16,'pool'=2,'dp'=8] {'seq'}, dimensions={0} | all-to-all | bytes 1048576 | tf_op jit(solution)/shard_map/all_to_all | solution.py:116
  361.1 3.7 all-to-all-start.6
  364.8 26.7 %collective-permute-start.2 = (bf16[32,512]{1,0:T(8,128)(2,1)S(1)}, bf16[32,512]{1,0:T(8,128)(2,1)S(1)}, u32[]{:S(2)}, u32[]{:S(2)}) collective-permute-start(bf16[32,512]{1,0:T(8,128)(2,1)S(1)} %copy_bitcast_fusion.10), channel_id=1, source_target_pairs={{0,8},{8,0},{1,9},{9,1},{2,10},{10,2},{3,11},{11,3},{4,12},{12,4},... | collective-permute-start | bytes 98312 | tf_op jit(solution)/shard_map/ppermute | solution.py:23
  391.6 20.0 %collective-permute-done.2 = bf16[32,512]{1,0:T(8,128)(2,1)S(1)} collective-permute-done((bf16[32,512]{1,0:T(8,128)(2,1)S(1)}, bf16[32,512]{1,0:T(8,128)(2,1)S(1)}, u32[]{:S(2)}, u32[]{:S(2)}) %collective-permute-start.2) | collective-permute-done | bytes 32800 | tf_op jit(solution)/shard_map/ppermute | solution.py:23
  412.1 166.4 %reduce-scatter.2.cloned.1.call-done = bf16[256,512]{0,1:T(8,128)(2,1)} async-done(((bf16[8192,512]{0,1:T(8,128)(2,1)}), bf16[256,512]{0,1:T(8,128)(2,1)}) %reduce-scatter.2.cloned.1.call-update) | async-done | bytes 262160 | tf_op jit(solution)/shard_map/reduce_scatter | solution.py:128
  582.6 2.3 copy.93
  584.9 61.1 %all-reduce.2.cloned.1.call-done = bf16[256,512]{0,1:T(8,128)(2,1)} async-done(((bf16[256,512]{0,1:T(8,128)(2,1)}), bf16[256,512]{0,1:T(8,128)(2,1)}) %all-reduce.2.cloned.1.call-update) | async-done | bytes 262160 | tf_op jit(solution)/shard_map/psum | solution.py:137
  (143 shorter events, 64.2 us)
Async XLA Ops:
  7.2 299.5 %copy-start = (bf16[1,1,128,8192]{3,2,1,0:T(8,128)(2,1)S(1)}, bf16[1,1,128,8192]{3,2,1,0:T(8,128)(2,1)}, u32[]{:S(2)}) copy-start(bf16[1,1,128,8192]{3,2,1,0:T(8,128)(2,1)} %param.16) | copy-start | bytes 6291460
  7.2 4.1 collective-permute-start.1
  9.7 12.9 %collective-permute-start = (bf16[32,512]{1,0:T(8,128)(2,1)}, bf16[32,512]{1,0:T(8,128)(2,1)S(1)}, u32[]{:S(2)}, u32[]{:S(2)}) collective-permute-start(bf16[32,512]{1,0:T(8,128)(2,1)} %bitcast.221), channel_id=1, source_target_pairs={{0,8},{8,0},{1,9},{9,1},{2,10},{10,2},{3,11},{11,3},{4,12},{12,4},... | collective-permute-start | bytes 98312 | tf_op jit(solution)/shard_map/ppermute | solution.py:23
  11.9 20.4 %all-to-all-start.4 = ((bf16[32,16,128]{2,0,1:T(8,128)(2,1)}), bf16[32,16,128]{2,0,1:T(8,128)(2,1)S(1)}, u32[]{:S(2)}, u32[]{:S(2)}) async-start(bf16[32,16,128]{2,0,1:T(8,128)(2,1)} %bitcast.13), calls=%async_computation.4 | async-start | bytes 262144 | tf_op jit(solution)/shard_map/all_to_all | solution.py:55
  33.0 13.1 %all-to-all-start.1 = ((bf16[32,16,128]{2,0,1:T(8,128)(2,1)}), bf16[32,16,128]{2,0,1:T(8,128)(2,1)S(1)}, u32[]{:S(2)}, u32[]{:S(2)}) async-start(bf16[32,16,128]{2,0,1:T(8,128)(2,1)} %bitcast.4), calls=%async_computation.1 | async-start | bytes 262144 | tf_op jit(solution)/shard_map/all_to_all | solution.py:54
  46.0 0.9 copy-start.11
  46.9 17.1 %all-to-all-start.5 = ((bf16[128,16,128]{2,0,1:T(8,128)(2,1)}), bf16[128,16,128]{2,0,1:T(8,128)(2,1)S(1)}, u32[]{:S(2)}, u32[]{:S(2)}) async-start(bf16[128,16,128]{2,0,1:T(8,128)(2,1)} %bitcast.16), calls=%async_computation.5 | async-start | bytes 1048576 | tf_op jit(solution)/shard_map/all_to_all | solution.py:53
  64.1 18.0 %copy-start.7 = (bf16[128,16,128]{2,0,1:T(8,128)(2,1)}, bf16[128,16,128]{2,0,1:T(8,128)(2,1)S(1)}, u32[]{:S(2)}) copy-start(bf16[128,16,128]{2,0,1:T(8,128)(2,1)S(1)} %all-to-all-done.5) | copy-start | bytes 1572868
  65.0 17.1 %all-to-all-start.2 = ((bf16[128,16,128]{0,2,1:T(8,128)(2,1)}), bf16[128,16,128]{0,2,1:T(8,128)(2,1)S(1)}, u32[]{:S(2)}, u32[]{:S(2)}) async-start(bf16[128,16,128]{0,2,1:T(8,128)(2,1)} %bitcast.8), calls=%async_computation.2 | async-start | bytes 1048576 | tf_op jit(solution)/shard_map/all_to_all | solution.py:52
  72.2 40.8 %copy-start.16 = (s32[1,1,2,4]{3,2,1,0:T(2,128)S(1)}, s32[1,1,2,4]{3,2,1,0:T(2,128)}, u32[]{:S(2)}) copy-start(s32[1,1,2,4]{3,2,1,0:T(2,128)} %param.17) | copy-start | bytes 100
  82.1 0.8 copy-start.8
  82.9 24.4 %all-to-all-start = ((bf16[128,16,256]{2,0,1:T(8,128)(2,1)}), bf16[128,16,256]{2,0,1:T(8,128)(2,1)S(1)}, u32[]{:S(2)}, u32[]{:S(2)}) async-start(bf16[128,16,256]{2,0,1:T(8,128)(2,1)} %copy.76), calls=%async_computation | async-start | bytes 2097152 | tf_op jit(solution)/shard_map/all_to_all | solution.py:47
  107.3 5.7 copy-start.4
  107.3 22.8 %all-to-all-start.3 = ((bf16[128,16,256]{2,0,1:T(8,128)(2,1)}), bf16[128,16,256]{2,0,1:T(8,128)(2,1)}, u32[]{:S(2)}, u32[]{:S(2)}) async-start(bf16[128,16,256]{2,0,1:T(8,128)(2,1)} %copy.80), calls=%async_computation.3 | async-start | bytes 2097152 | tf_op jit(solution)/shard_map/all_to_all | solution.py:48
  112.9 465.6 %reduce-scatter.2.cloned.1.call-start = ((), (), s32[]{:S(2)}) async-start(), calls=%async_computation.12 | async-start | bytes 8650752 | tf_op jit(solution)/shard_map/reduce_scatter | solution.py:128
  151.2 7.1 %copy-start.1 = (f32[2,512,2560]{2,1,0:T(8,128)S(1)}, f32[2,512,2560]{2,1,0:T(8,128)}, u32[]{:S(2)}) copy-start(f32[2,512,2560]{2,1,0:T(8,128)} %get-tuple-element.354) | copy-start | bytes 31457284 | tf_op jit(solution)/shard_map/while
  151.2 7.2 %copy-start.3 = (bf16[1,512,2,128]{3,2,1,0:T(2,128)(2,1)S(1)}, bf16[1,512,2,128]{3,2,1,0:T(2,128)(2,1)}, u32[]{:S(2)}) copy-start(bf16[1,512,2,128]{3,2,1,0:T(2,128)(2,1)} %get-tuple-element.356) | copy-start | bytes 786436 | tf_op jit(solution)/shard_map/while
  151.2 7.7 %copy-start.10 = (bf16[2560,128]{1,0:T(8,128)(2,1)S(1)}, bf16[2560,128]{1,0:T(8,128)(2,1)}, u32[]{:S(2)}) copy-start(bf16[2560,128]{1,0:T(8,128)(2,1)} %get-tuple-element.394) | copy-start | bytes 1966084 | tf_op jit(solution)/shard_map/while
  160.9 1.8 copy-start.9
  162.6 2.5 copy-start.2
  189.7 7.4 %copy-start.1 = (f32[2,512,2560]{2,1,0:T(8,128)S(1)}, f32[2,512,2560]{2,1,0:T(8,128)}, u32[]{:S(2)}) copy-start(f32[2,512,2560]{2,1,0:T(8,128)} %get-tuple-element.354) | copy-start | bytes 31457284 | tf_op jit(solution)/shard_map/while
  189.7 7.5 %copy-start.3 = (bf16[1,512,2,128]{3,2,1,0:T(2,128)(2,1)S(1)}, bf16[1,512,2,128]{3,2,1,0:T(2,128)(2,1)}, u32[]{:S(2)}) copy-start(bf16[1,512,2,128]{3,2,1,0:T(2,128)(2,1)} %get-tuple-element.356) | copy-start | bytes 786436 | tf_op jit(solution)/shard_map/while
  189.7 8.0 %copy-start.10 = (bf16[2560,128]{1,0:T(8,128)(2,1)S(1)}, bf16[2560,128]{1,0:T(8,128)(2,1)}, u32[]{:S(2)}) copy-start(bf16[2560,128]{1,0:T(8,128)(2,1)} %get-tuple-element.394) | copy-start | bytes 1966084 | tf_op jit(solution)/shard_map/while
  199.8 1.8 copy-start.9
  201.5 2.5 copy-start.2
  228.7 7.4 %copy-start.1 = (f32[2,512,2560]{2,1,0:T(8,128)S(1)}, f32[2,512,2560]{2,1,0:T(8,128)}, u32[]{:S(2)}) copy-start(f32[2,512,2560]{2,1,0:T(8,128)} %get-tuple-element.354) | copy-start | bytes 31457284 | tf_op jit(solution)/shard_map/while
  228.7 7.5 %copy-start.3 = (bf16[1,512,2,128]{3,2,1,0:T(2,128)(2,1)S(1)}, bf16[1,512,2,128]{3,2,1,0:T(2,128)(2,1)}, u32[]{:S(2)}) copy-start(bf16[1,512,2,128]{3,2,1,0:T(2,128)(2,1)} %get-tuple-element.356) | copy-start | bytes 786436 | tf_op jit(solution)/shard_map/while
  228.7 8.0 %copy-start.10 = (bf16[2560,128]{1,0:T(8,128)(2,1)S(1)}, bf16[2560,128]{1,0:T(8,128)(2,1)}, u32[]{:S(2)}) copy-start(bf16[2560,128]{1,0:T(8,128)(2,1)} %get-tuple-element.394) | copy-start | bytes 1966084 | tf_op jit(solution)/shard_map/while
  238.7 1.8 copy-start.9
  240.5 2.5 copy-start.2
  267.6 7.4 %copy-start.1 = (f32[2,512,2560]{2,1,0:T(8,128)S(1)}, f32[2,512,2560]{2,1,0:T(8,128)}, u32[]{:S(2)}) copy-start(f32[2,512,2560]{2,1,0:T(8,128)} %get-tuple-element.354) | copy-start | bytes 31457284 | tf_op jit(solution)/shard_map/while
  267.6 7.5 %copy-start.3 = (bf16[1,512,2,128]{3,2,1,0:T(2,128)(2,1)S(1)}, bf16[1,512,2,128]{3,2,1,0:T(2,128)(2,1)}, u32[]{:S(2)}) copy-start(bf16[1,512,2,128]{3,2,1,0:T(2,128)(2,1)} %get-tuple-element.356) | copy-start | bytes 786436 | tf_op jit(solution)/shard_map/while
  267.6 8.0 %copy-start.10 = (bf16[2560,128]{1,0:T(8,128)(2,1)S(1)}, bf16[2560,128]{1,0:T(8,128)(2,1)}, u32[]{:S(2)}) copy-start(bf16[2560,128]{1,0:T(8,128)(2,1)} %get-tuple-element.394) | copy-start | bytes 1966084 | tf_op jit(solution)/shard_map/while
  277.6 1.8 copy-start.9
  279.4 2.5 copy-start.2
  288.9 0.9 copy-start.5
  312.4 0.8 copy-start.6
  313.9 13.1 %all-to-all-start.9 = ((bf16[16,32,128]{2,1,0:T(8,128)(2,1)}), bf16[16,32,128]{2,1,0:T(8,128)(2,1)S(1)}, u32[]{:S(2)}, u32[]{:S(2)}) async-start(bf16[16,32,128]{2,1,0:T(8,128)(2,1)} %bitcast.30), calls=%async_computation.9 | async-start | bytes 262144 | tf_op jit(solution)/shard_map/all_to_all | solution.py:118
  326.9 15.7 %all-to-all-start.10 = ((bf16[16,32,128]{2,1,0:T(8,128)(2,1)}), bf16[16,32,128]{2,1,0:T(8,128)(2,1)S(1)}, u32[]{:S(2)}, u32[]{:S(2)}) async-start(bf16[16,32,128]{2,1,0:T(8,128)(2,1)} %bitcast.34), calls=%async_computation.10 | async-start | bytes 262144 | tf_op jit(solution)/shard_map/all_to_all | solution.py:119
  361.1 220.3 %all-to-all-start.6 = ((bf16[16,128,256]{2,1,0:T(8,128)(2,1)}), bf16[16,128,256]{2,1,0:T(8,128)(2,1)S(1)}, u32[]{:S(2)}, u32[]{:S(2)}) async-start(bf16[16,128,256]{2,1,0:T(8,128)(2,1)} %bitcast.213), calls=%async_computation.6 | async-start | bytes 2097152 | tf_op jit(solution)/shard_map/all_to_all | solution.py:110
  364.7 281.3 %all-reduce.2.cloned.1.call-start = ((), (), s32[]{:S(2)}) async-start(), calls=%async_computation.13 | async-start | bytes 524288 | tf_op jit(solution)/shard_map/psum | solution.py:137
  364.8 46.8 %collective-permute-start.2 = (bf16[32,512]{1,0:T(8,128)(2,1)S(1)}, bf16[32,512]{1,0:T(8,128)(2,1)S(1)}, u32[]{:S(2)}, u32[]{:S(2)}) collective-permute-start(bf16[32,512]{1,0:T(8,128)(2,1)S(1)} %copy_bitcast_fusion.10), channel_id=1, source_target_pairs={{0,8},{8,0},{1,9},{9,1},{2,10},{10,2},{3,11},{11,3},{4,12},{12,4},... | collective-permute-start | bytes 98312 | tf_op jit(solution)/shard_map/ppermute | solution.py:23
  391.5 20.6 %collective-permute-start.3 = (bf16[32,512]{1,0:T(8,128)(2,1)S(1)}, bf16[32,512]{1,0:T(8,128)(2,1)S(1)}, u32[]{:S(2)}, u32[]{:S(2)}) collective-permute-start(bf16[32,512]{1,0:T(8,128)(2,1)S(1)} %copy_bitcast_fusion.9), channel_id=1, source_target_pairs={{0,8},{8,0},{1,9},{9,1},{2,10},{10,2},{3,11},{11,3},{4,12},{12,4},... | collective-permute-start | bytes 98312 | tf_op jit(solution)/shard_map/ppermute | solution.py:23
  411.6 166.9 %copy-start.12 = (bf16[32,512]{1,0:T(8,128)(2,1)}, bf16[32,512]{1,0:T(8,128)(2,1)S(1)}, u32[]{:S(2)}) copy-start(bf16[32,512]{1,0:T(8,128)(2,1)S(1)} %collective-permute-done.2) | copy-start | bytes 98308
  412.1 166.4 %copy-start.14 = (bf16[32,512]{1,0:T(8,128)(2,1)}, bf16[32,512]{1,0:T(8,128)(2,1)S(1)}, u32[]{:S(2)}) copy-start(bf16[32,512]{1,0:T(8,128)(2,1)S(1)} %collective-permute-done.3) | copy-start | bytes 98308
  579.8 68.1 %copy-start.13 = (bf16[32,512]{1,0:T(8,128)(2,1)S(1)}, bf16[32,512]{1,0:T(8,128)(2,1)}, u32[]{:S(2)}) copy-start(bf16[32,512]{1,0:T(8,128)(2,1)} %copy-done.12) | copy-start | bytes 98308
  579.8 68.7 %copy-start.15 = (bf16[32,512]{1,0:T(8,128)(2,1)S(1)}, bf16[32,512]{1,0:T(8,128)(2,1)}, u32[]{:S(2)}) copy-start(bf16[32,512]{1,0:T(8,128)(2,1)} %copy-done.14) | copy-start | bytes 98308
Sparse Core Ops, SparseCore 0:
  312.4 266.0 reduce-scatter.1
  580.9 65.0 all-reduce.1
where the time goes:
time: 659 us; the launch traced here: 656 us
  waiting for transfers between devices  329 us (50%)
  matrix products  105 us (16%)
  starting transfers between devices  75.9 us (12%)
  local copies, waits for them, and re-layouts  68.8 us (10%)
  blocking collectives  33.4 us (5%)
  other arithmetic  26.6 us (4%)
  between operations  14.3 us (2%)
    reduce_scatter x1, waiting for transfers between devices, on_device(): lax.psum_scatter(lax.dot_general(tokens_in, value_grad, (((0,), (0,)), ((...  166 us
    psum x1, waiting for transfers between devices, on_device(): lax.psum(shard, 'dp').astype(jnp.float32) / ranks  61.1 us
    sub x4, matrix products, step(): expo = jnp.exp(scores - top)  38.2 us
    ppermute x4, starting transfers between devices, swapped(): return lax.ppermute(block, axis, route)  29.4 us
    dot_general x4, matrix products, step(): jnp.einsum('hqk,qhd->kd', probs_low, g_part, preferred_element_type=jnp.f...  29.3 us
    ppermute x4, waiting for transfers between devices, swapped(): return lax.ppermute(block, axis, route)  21.9 us
    all_to_all x1, blocking collectives, on_device(): lax.all_to_all(part_k[past:], 'seq', split_axis=0, concat_axis=1, tiled=T...  18.4 us
    all_to_all x1, waiting for transfers between devices, on_device(): lax.all_to_all(queries[0, 0], 'seq', split_axis=1, concat_axis=0, tiled=T...  16.3 us
  transfers between devices with their start and end apart: 15, of which 13 were waited for; matrix products, arithmetic and copies ran while one was open for 4% of the time, Pallas kernels for 0%

commit v1 on v0

v1 whole, which is shorter than its diff:
```python
import jax
import jax.numpy as jnp
from jax import lax
from jax.experimental import pallas as pl
from jax.experimental.pallas import tpu as pltpu
from jax.sharding import PartitionSpec as P

MESH = pl.DeviceIdType.MESH
BF = jnp.bfloat16
F32 = jnp.float32
HD = 128
NY = 4
NJ = 4
NDP = 8
TOK = 128
OLDT = 32
ROWS = 1024
CHUNK = 512
SCALE = HD**-0.5
EXPC = SCALE * 1.4426950408889634
NEG = -1e30
UNITS = [(i, c) for i in range(4) for c in range(i + 2)]
UNIT = {u: n for n, u in enumerate(UNITS)}


def dot(a, b):
    return jnp.dot(a, b, preferred_element_type=F32)


def dot_nt(a, b):
    return lax.dot_general(a, b, (((1,), (1,)), ((), ())), preferred_element_type=F32)


def kernel(
    q_ref, k_ref, v_ref, ok_ref, ov_ref, g_ref, x_ref, bias_ref,
    dq_ref, dk_ref, dv_ref, odk_ref, odv_ref, dw_ref,
    xin, xloc, xall, qb, gb, kc, ko, kst, kt, ebuf, sbuf, linv, gl, ql, dqb,
    part, opart, oown, cown, m1, m2, m3, mrg, rold, vg4, og4, vgall,
    wp, wown, ry, wz, rz, wfin, ssem, rsem, lsem,
):
    seq = lax.axis_index("seq")
    p = lax.axis_index("pool")
    dp = lax.axis_index("dp")
    y = seq // NJ
    j = seq % NJ
    z = 2 * j + p
    x = dp // 2
    core = dp % 2
    jr = (j + 1) % NJ
    jl = (j + 3) % NJ
    jo = (j + 2) % NJ

    def at_y(yy):
        return (yy * NJ + j, p, dp)

    def at_j(jj, pp=None):
        return (y * NJ + jj, p if pp is None else pp, dp)

    def at_dp(dd):
        return (seq, p, dd)

    count = {"s": 0, "r": 0, "l": 0}
    sends = []

    def take(kind, n=1):
        base = count[kind]
        count[kind] += n
        return base

    def send(src, dst, rs, dev):
        c = pltpu.make_async_remote_copy(
            src_ref=src, dst_ref=dst, send_sem=ssem.at[take("s")], recv_sem=rsem.at[rs],
            device_id=dev, device_id_type=MESH,
        )
        c.start()
        sends.append(c)

    def arrived(dst, rs):
        pltpu.make_async_copy(dst, dst, rsem.at[rs]).wait()

    def local(src, dst):
        c = pltpu.make_async_copy(src, dst, lsem.at[take("l")])
        c.start()
        return c

    barrier = pltpu.get_barrier_semaphore()
    peers = [at_y((y + r) % NY) for r in range(1, NY)]
    peers += [at_j(((z + t) % 8) // 2, ((z + t) % 8) % 2) for t in range(1, 8)]
    peers += [at_dp((dp + t) % NDP) for t in range(1, NDP)]
    for dev in peers:
        pl.semaphore_signal(barrier, inc=1, device_id=dev, device_id_type=MESH)
    pl.semaphore_wait(barrier, len(peers))

    def col(n, width=HD):
        return pl.ds(pl.multiple_of(n * width, width), width)

    r_kv = [[take("r") for _ in range(3)] for _ in range(2)]
    r_ov = [[take("r") for _ in range(3)] for _ in range(2)]
    r_q = take("r", 4)
    r_g = take("r", 4)
    loc_x = local(x_ref, xin)
    loc_kv = []
    for a, (cur, old) in enumerate(((k_ref, ok_ref), (v_ref, ov_ref))):
        loc_kv.append((local(cur.at[:, col(y)], kc.at[a, y, j]), local(old.at[:, col(y)], kst.at[a, y])))
        for r in range(1, NY):
            yy = (y + r) % NY
            send(cur.at[:, col(yy)], kc.at[a, y, j], r_kv[a][r - 1], at_y(yy))
            send(old.at[:, col(yy)], kst.at[a, y], r_ov[a][r - 1], at_y(yy))
    loc_q = local(q_ref.at[:, col(y, ROWS)], qb.at[y])
    loc_g = local(g_ref.at[:, col(y, ROWS)], gb.at[y])
    for r in range(1, NY):
        yy = (y + r) % NY
        send(q_ref.at[:, col(yy, ROWS)], qb.at[y], r_q + r, at_y(yy))

    r_side = [[take("r"), take("r")] for _ in range(2)]
    r_fwd = [[take("r"), take("r")] for _ in range(2)]
    r_oz = [take("r", 4) for _ in range(2)]

    def gather_start(a):
        loc_kv[a][0].wait()
        loc_kv[a][1].wait()
        for r in range(1, NY):
            yy = (y + NY - r) % NY
            arrived(kc.at[a, yy, j], r_kv[a][r - 1])
            arrived(kst.at[a, yy], r_ov[a][r - 1])
        send(kc.at[a, :, j], kc.at[a, :, j], r_side[a][0], at_j(jr))
        send(kc.at[a, :, j], kc.at[a, :, j], r_side[a][1], at_j(jl))
        for t in range(NJ):
            jj = (j + t) % NJ
            send(kst.at[a], ko.at[a, :, j], r_oz[a] + t, at_j(jj, 1 - p))

    def gather_forward(a):
        arrived(kc.at[a, :, jl], r_side[a][0])
        send(kc.at[a, 0:2, jl], kc.at[a, 0:2, jl], r_fwd[a][0], at_j(jr))
        arrived(kc.at[a, :, jr], r_side[a][1])
        send(kc.at[a, 2:4, jr], kc.at[a, 2:4, jr], r_fwd[a][1], at_j(jl))

    def gather_end(a):
        arrived(kc.at[a, 0:2, jo], r_fwd[a][0])
        arrived(kc.at[a, 2:4, jo], r_fwd[a][1])
        for t in range(NJ):
            arrived(ko.at[a, :, (j + NJ - t) % NJ], r_oz[a] + t)

    def chunk(a, c):
        if c == 0:
            return ko[a].reshape(CHUNK, HD)
        return kc[a, c - 1].reshape(CHUNK, HD)

    gather_start(0)

    loc_x.wait()

    def turn(b, _):
        for half in range(2):
            block = xin[:, pl.ds(pl.multiple_of(b * 256 + half * 128, 128), 128)]
            xloc[b, pl.ds(half * 4, 4)] = block.T.reshape(4, 32, TOK)
        return 0

    lax.fori_loop(0, 32, turn, 0)
    r_x = take("r", 8)
    loc_xx = local(xloc.at[:, dp], xall.at[:, :, col(dp)])
    for t in range(1, NDP):
        dd = (dp + t) % NDP
        send(xloc.at[:, dd], xall.at[:, :, col(dp)], r_x + t, at_dp(dd))

    gather_forward(0)
    gather_start(1)
    loc_q.wait()
    for r in range(1, NY):
        arrived(qb.at[(y + NY - r) % NY], r_q + r)
    for r in range(1, NY):
        yy = (y + r) % NY
        send(g_ref.at[:, col(yy, ROWS)], gb.at[y], r_g + r, at_y(yy))
    gather_end(0)
    for c in range(5):
        kt[c] = chunk(0, c).T

    def heads(ref, i, hp):
        block = ref[i, :, pl.ds(pl.multiple_of(hp * 256, 256), 256)]
        return jnp.concatenate([block[:, :HD], block[:, HD:]], axis=0)

    def lanes(hp):
        return pl.ds(pl.multiple_of(hp * 256, 256), 256)

    def probs(i):
        def body(hp, _):
            qh = heads(qb, i, hp)
            top = None
            for c in range(i + 2):
                s = dot_nt(chunk(0, c), qh)
                if c == 0:
                    s = jnp.concatenate(
                        [s[n * 128:(n + 1) * 128] + bias_ref[i // 2, n] for n in range(4)], axis=0
                    )
                elif c == i + 1:
                    ahead = lax.broadcasted_iota(jnp.int32, s.shape, 0) - lax.broadcasted_iota(
                        jnp.int32, s.shape, 1
                    ) % TOK
                    s = jnp.where(ahead <= TOK * j, s, NEG)
                sbuf[c] = s
                high = jnp.max(s, axis=0, keepdims=True)
                top = high if top is None else jnp.maximum(top, high)
            total = None
            for c in range(i + 2):
                e = jnp.exp2((sbuf[c] - top) * EXPC)
                add = jnp.sum(e, axis=0, keepdims=True)
                total = add if total is None else total + add
                ebuf[UNIT[i, c], :, lanes(hp)] = e.astype(BF)
            linv[i, :, lanes(hp)] = 1.0 / total
            return 0

        lax.fori_loop(0, 4, body, 0)

    probs(0)
    probs(1)
    gather_forward(1)
    probs(2)
    probs(3)

    loc_g.wait()
    for r in range(1, NY):
        arrived(gb.at[(y + NY - r) % NY], r_g + r)

    def spread(n, _):
        i = n // 8
        h = n % 8
        at = pl.ds(pl.multiple_of(h * HD, HD), HD)
        inv = jnp.broadcast_to(linv[i, :, at], (HD, HD)).T
        gl[i, at, :] = (gb[i, :, at].astype(F32) * inv).astype(BF)
        ql[i, at, :] = (qb[i, :, at].astype(F32) * (inv * SCALE)).astype(BF)
        return 0

    lax.fori_loop(0, 32, spread, 0)

    def keys_grad(a, right):
        for c in range(5):
            first = max(c - 1, 0)
            acc = None
            for i in range(first, 4):
                term = dot(ebuf[UNIT[i, c]], right[i])
                acc = term if acc is None else acc + term
            if c == 0:
                opart[a] = acc.astype(BF).reshape(NY, NJ, OLDT, HD)
            else:
                part[a, c - 1] = acc.astype(BF).reshape(NJ, TOK, HD)

    r_m1 = [[take("r"), take("r")] for _ in range(2)]
    r_m2 = [[take("r"), take("r")] for _ in range(2)]
    r_m3 = [[take("r"), take("r")] for _ in range(2)]
    r_old = [take("r", 4) for _ in range(2)]

    def sum_start(a):
        send(part.at[a, 0:2, jo], m1.at[a, 0], r_m1[a][0], at_j(jr))
        send(part.at[a, 2:4, jo], m1.at[a, 1], r_m1[a][1], at_j(jl))
        send(part.at[a, 2:4, jr], m2.at[a, 1], r_m2[a][0], at_j(jr))
        send(part.at[a, 0:2, jl], m2.at[a, 0], r_m2[a][1], at_j(jl))
        for t in range(NJ):
            jj = (j + t) % NJ
            send(opart.at[a, :, jj], rold.at[a, t], r_old[a] + t, at_j(jj, 1 - p))

    def sum_merge(a):
        arrived(m1.at[a, 0], r_m1[a][0])
        mrg[a, 0] = (m1[a, 0].astype(F32) + part[a, 0:2, jr].astype(F32)).astype(BF)
        send(mrg.at[a, 0], m3.at[a, 0], r_m3[a][0], at_j(jr))
        arrived(m1.at[a, 1], r_m1[a][1])
        mrg[a, 1] = (m1[a, 1].astype(F32) + part[a, 2:4, jl].astype(F32)).astype(BF)
        send(mrg.at[a, 1], m3.at[a, 1], r_m3[a][1], at_j(jl))

    r_fin = [take("r", 4) for _ in range(2)]
    r_ofin = [take("r", 4) for _ in range(2)]

    def sum_end(a, here, put, oput):
        arrived(m2.at[a, 1], r_m2[a][0])
        arrived(m2.at[a, 0], r_m2[a][1])
        arrived(m3.at[a, 0], r_m3[a][0])
        arrived(m3.at[a, 1], r_m3[a][1])
        for half in range(2):
            vg4[a, pl.ds(half * 2, 2)] = (
                part[a, pl.ds(half * 2, 2), j].astype(F32)
                + m2[a, half].astype(F32)
                + m3[a, half].astype(F32)
            ).astype(BF)
        own = local(vg4.at[a, y], put)
        for r in range(1, NY):
            yy = (y + r) % NY
            send(vg4.at[a, yy], put, r_fin[a] + r, at_y(yy))
        for t in range(NJ):
            arrived(rold.at[a, t], r_old[a] + t)
        og4[a] = (
            rold[a, 0].astype(F32) + rold[a, 1].astype(F32)
            + rold[a, 2].astype(F32) + rold[a, 3].astype(F32)
        ).astype(BF)
        oown_copy = local(og4.at[a, y], oput)
        for r in range(1, NY):
            yy = (y + r) % NY
            send(og4.at[a, yy], oput, r_ofin[a] + r, at_y(yy))
        return own, oown_copy

    def sum_arrived(a, copies, whole, owhole):
        copies[0].wait()
        copies[1].wait()
        for r in range(1, NY):
            yy = (y + NY - r) % NY
            arrived(whole.at[:, col(yy)], r_fin[a] + r)
            arrived(owhole.at[:, col(yy)], r_ofin[a] + r)

    keys_grad(1, gl)
    sum_start(1)

    gather_end(1)
    r_dq = take("r", 4)

    def scores_grad(i):
        def body(hp, _):
            gh = heads(gb, i, hp)
            inv = linv[i, :, lanes(hp)]
            delta = None
            for c in range(i + 2):
                d = dot_nt(chunk(1, c), gh)
                sbuf[c] = d
                add = jnp.sum(ebuf[UNIT[i, c], :, lanes(hp)].astype(F32) * d, axis=0, keepdims=True)
                delta = add if delta is None else delta + add
            delta = delta * inv
            acc = None
            for c in range(i + 2):
                t = (ebuf[UNIT[i, c], :, lanes(hp)].astype(F32) * (sbuf[c] - delta)).astype(BF)
                ebuf[UNIT[i, c], :, lanes(hp)] = t
                term = dot(kt[c], t)
                acc = term if acc is None else acc + term
            acc = acc * (inv * SCALE)
            out = jnp.concatenate([acc[:, :HD].T, acc[:, HD:].T], axis=1)
            dqb[i, :, lanes(hp)] = out.astype(BF)
            return 0

        lax.fori_loop(0, 4, body, 0)

    scores_grad(0)
    sum_merge(1)
    scores_grad(1)
    vcopies = sum_end(1, dv_ref, vgall.at[dp, :, col(y)], odv_ref.at[:, col(y)])
    scores_grad(2)
    sum_arrived(1, vcopies, vgall.at[dp], odv_ref)
    r_vg = take("r", 4)
    r_vs = take("r", 4)
    dv_copy = local(vgall.at[dp], dv_ref)
    sib = 2 * x + 1 - core
    send(vgall.at[dp], vgall.at[dp], r_vs, at_dp(sib))
    for t in range(1, 4):
        send(vgall.at[dp], vgall.at[dp], r_vg + t, at_dp(2 * ((x + t) % 4) + core))
    scores_grad(3)
    loc_dq = local(dqb.at[y], dq_ref.at[:, col(y, ROWS)])
    for r in range(1, NY):
        yy = (y + r) % NY
        send(dqb.at[yy], dq_ref.at[:, col(y, ROWS)], r_dq + r, at_y(yy))
    for t in range(1, 4):
        d = 2 * ((x + 4 - t) % 4) + core
        arrived(vgall.at[d], r_vg + t)
        send(vgall.at[d], vgall.at[d], r_vs + t, at_dp(sib))
    keys_grad(0, ql)
    sum_start(0)

    loc_xx.wait()
    for t in range(1, NDP):
        arrived(xall.at[:, :, col((dp + NDP - t) % NDP)], r_x + t)
    for t in range(4):
        arrived(vgall.at[2 * ((x + 4 - t) % 4) + 1 - core], r_vs + t)
    r_wy = take("r", 4)

    def weight(yy):
        left = xall[pl.ds(yy * 8, 8)].reshape(256, NDP * TOK)
        return dot(left, vgall[...].reshape(NDP * TOK, 4 * HD)).reshape(8, 32, 4 * HD)

    for r in range(1, NY):
        yy = (y + r) % NY
        wp[r - 1] = weight(yy).astype(BF)
        send(wp.at[r - 1], ry.at[r - 1], r_wy + r, at_y(yy))
    sum_merge(0)
    wown[...] = weight(y)
    kcopies = sum_end(0, dk_ref, dk_ref.at[:, col(y)], odk_ref.at[:, col(y)])
    for r in range(1, NY):
        arrived(ry.at[r - 1], r_wy + r)
    wz[...] = (
        wown[...] + ry[0].astype(F32) + ry[1].astype(F32) + ry[2].astype(F32)
    ).astype(BF)
    r_wz = take("r", 8)
    for t in range(1, 8):
        zz = (z + t) % 8
        send(wz.at[zz], rz.at[t - 1], r_wz + t, at_j(zz // 2, zz % 2))
    acc = wz[z].astype(F32)
    for t in range(1, 8):
        arrived(rz.at[t - 1], r_wz + t)
        acc = acc + rz[t - 1].astype(F32)
    wfin[...] = (acc * (1.0 / 256.0)).astype(BF)
    r_wd = take("r", 8)
    rows = pl.ds(pl.multiple_of(dp * 32, 32), 32)
    own_w = local(wfin, dw_ref.at[rows])
    for t in range(1, NDP):
        send(wfin, dw_ref.at[rows], r_wd + t, at_dp((dp + t) % NDP))

    sum_arrived(0, kcopies, dk_ref, odk_ref)
    dv_copy.wait()
    loc_dq.wait()
    for r in range(1, NY):
        arrived(dq_ref.at[:, col((y + NY - r) % NY, ROWS)], r_dq + r)
    own_w.wait()
    for t in range(1, NDP):
        d = (dp + NDP - t) % NDP
        arrived(dw_ref.at[pl.ds(pl.multiple_of(d * 32, 32), 32)], r_wd + t)
    for c in sends:
        c.wait_send()
    assert count["s"] <= ssem.shape[0] and count["r"] <= rsem.shape[0]
    assert count["l"] <= lsem.shape[0]


def on_device(queries, keys, values, old_keys, old_values, out_grad, inputs, reads):
    bias = (jnp.minimum(reads[0, 0], 1).astype(F32) - 1.0) * (-NEG)
    anywhere = pl.BlockSpec(memory_space=pl.ANY)
    out = [(TOK, 4096), (TOK, 512), (TOK, 512), (OLDT, 512), (OLDT, 512), (256, 512)]
    bf = lambda *shape: pltpu.VMEM(shape, BF)
    f32 = lambda *shape: pltpu.VMEM(shape, F32)
    results = pl.pallas_call(
        kernel,
        out_shape=[jax.ShapeDtypeStruct(shape, BF) for shape in out],
        in_specs=[anywhere] * 7 + [pl.BlockSpec(memory_space=pltpu.SMEM)],
        out_specs=[anywhere] * 6,
        scratch_shapes=[
            bf(TOK, 8192),
            bf(32, 8, 32, TOK),
            bf(32, 32, NDP * TOK),
            bf(4, TOK, ROWS),
            bf(4, TOK, ROWS),
            bf(2, NY, NJ, TOK, HD),
            bf(2, NY, NJ, OLDT, HD),
            bf(2, NY, OLDT, HD),
            bf(5, HD, CHUNK),
            bf(len(UNITS), CHUNK, ROWS),
            f32(5, CHUNK, 256),
            f32(4, 1, ROWS),
            bf(4, ROWS, HD),
            bf(4, ROWS, HD),
            bf(4, TOK, ROWS),
            bf(2, NY, NJ, TOK, HD),
            bf(2, NY, NJ, OLDT, HD),
            bf(16, 128),
            bf(16, 128),
            bf(2, 2, 2, TOK, HD),
            bf(2, 2, 2, TOK, HD),
            bf(2, 2, 2, TOK, HD),
            bf(2, 2, 2, TOK, HD),
            bf(2, NJ, NY, OLDT, HD),
            bf(2, NY, TOK, HD),
            bf(2, NY, OLDT, HD),
            bf(NDP, TOK, 512),
            bf(3, 8, 32, 512),
            f32(8, 32, 512),
            bf(3, 8, 32, 512),
            bf(8, 32, 512),
            bf(7, 32, 512),
            bf(32, 512),
            pltpu.SemaphoreType.DMA((112,)),
            pltpu.SemaphoreType.DMA((128,)),
            pltpu.SemaphoreType.DMA((24,)),
        ],
        compiler_params=pltpu.CompilerParams(
            collective_id=0, has_side_effects=True, vmem_limit_bytes=56 * 1024 * 1024
        ),
        cost_estimate=pl.CostEstimate(
            flops=11_000_000_000, bytes_accessed=10_000_000, transcendentals=8_000_000
        ),
    )(
        queries[0, 0], keys[0, 0], values[0, 0], old_keys[0, 0], old_values[0, 0],
        out_grad[0, 0], inputs[0, 0], bias,
    )
    return tuple(r[None, None] for r in results[:5]) + (results[5],)


def solution(mesh):
    token = P("dp", "pool", "seq", None)
    in_specs = (token,) * 7 + (P("dp", "pool", None, None),)
    out_specs = (token,) * 5 + (P(("seq", "pool"), None),)
    return jax.shard_map(
        on_device, mesh=mesh, in_specs=in_specs, out_specs=out_specs, check_vma=False
    )
```

time: 659 us -> 117 us (0.18)
  waiting for transfers between devices: 329 us -> 0 us
  Pallas kernels: 0 us -> 109 us
  matrix products: 105 us -> 0 us
  starting transfers between devices: 75.9 us -> 0 us
  local copies, waits for them, and re-layouts: 68.8 us -> 5.62 us
  blocking collectives: 33.4 us -> 0 us
  other arithmetic: 26.6 us -> 1.25 us
  between operations: 14.3 us -> 0.69 us
    reduce_scatter x1 -> x0, waiting for transfers between devices: 166 us -> none  [on_device(): lax.psum_scatter(lax.dot_general(tokens_in, value_grad, (((0,), (0,)), ((...]
    pallas_call x0 -> x1, Pallas kernels: none -> 109 us  [on_device(): pl.pallas_call(kernel, out_shape=[jax.ShapeDtypeStruct(shape, BF) for sha...]
    all_to_all x9 -> x0, waiting for transfers between devices: 80 us -> none  [the longest x1 16.3 us: on_device(): lax.all_to_all(queries[0, 0], 'seq', split_axis=1, concat_axis=0, tiled=T...]
    dot_general x22 -> x0, matrix products: 66.3 us -> none  [the longest x4 29.3 us: step(): jnp.einsum('hqk,qhd->kd', probs_low, g_part, preferred_element_type=jnp.f...]
    psum x1 -> x0, waiting for transfers between devices: 61.1 us -> none  [on_device(): lax.psum(shard, 'dp').astype(jnp.float32) / ranks]
    all_to_all x9 -> x0, starting transfers between devices: 46.4 us -> none  [the longest x1 10.7 us: on_device(): lax.all_to_all(widen(held_v, copies), 'seq', split_axis=1, concat_axis=0,...]
    sub x4 -> x0, matrix products: 38.2 us -> none  [step(): expo = jnp.exp(scores - top)]
    all_to_all x2 -> x0, blocking collectives: 33.4 us -> none  [the longest x1 18.4 us: on_device(): lax.all_to_all(part_k[past:], 'seq', split_axis=0, concat_axis=1, tiled=T...]
  transfers between devices with their start and end apart: 15 -> 0, of which waited for: 13 -> 0; matrix products, arithmetic and copies ran while one was open for 4% -> 0% of each run, Pallas kernels for 0% -> 0%
where the time goes in v1:
time: 117 us
  Pallas kernels  109 us (93%)
  local copies, waits for them, and re-layouts  5.62 us (5%)
  other arithmetic  1.25 us (1%)
    pallas_call x1, Pallas kernels, on_device(): pl.pallas_call(kernel, out_shape=[jax.ShapeDtypeStruct(shape, BF) for sha...  109 us
    unnamed x16, local copies, waits for them, and re-layouts  5.62 us

profile of v1, /device:TPU:1, one launch (start us, length us, event | category | flops | bytes accessed | tf_op | source)
XLA Modules:
  0.0 116.8 jit_solution(14401878436657103622)
XLA Ops:
  0.6 1.2 %multiply_bitcast_fusion.bias_ref = f32[2,4]{1,0:T(2,128)} fusion(s32[1,1,2,4]{3,2,1,0:T(2,128)} %param.15), kind=kLoop, calls=%fused_computation | loop fusion | flops 32 | bytes 64 | tf_op jit(solution)/shard_map/mul | solution.py:416
  1.9 109.3 %shard_map.127 = (bf16[128,4096]{1,0:T(8,128)(2,1)}, bf16[128,512]{1,0:T(8,128)(2,1)}, bf16[128,512]{1,0:T(8,128)(2,1)}, bf16[32,512]{1,0:T(8,128)(2,1)}, bf16[3...) custom-call(bf16[128,4096]{1,0:T(8,128)(2,1)} %bitcast.20, bf16[128,512]{1,0:T(8,128)(2,1)} %bitcast.22, ...), custom_call_target="tpu_custom_call" | custom-call | flops 11000000512 | bytes 10000000 | tf_op jit(solution)/shard_map/pallas_call | solution.py:421
  111.2 0.0 copy-start.2
  111.2 0.0 copy-start.1
  111.2 0.0 copy-start.4
  111.2 0.0 copy-start.3
  111.2 0.0 copy-start
  111.2 2.4 %copy.20 = bf16[1,1,128,4096]{3,2,1,0:T(8,128)(2,1)} copy(bf16[1,1,128,4096]{3,2,1,0:T(8,128)(2,1)} %bitcast.14) | data formatting | bytes 2097152
  113.6 0.0 copy-done.2
  113.6 0.7 copy.21
  114.2 0.0 copy-done.1
  114.2 0.7 copy.22
  114.9 0.0 copy-done.4
  114.9 0.6 copy.23
  115.5 0.0 copy-done.3
  115.5 0.6 copy.24
  116.1 0.0 copy-done
  116.1 0.7 copy.25
Async XLA Ops:
  111.2 2.4 %copy-start.2 = (bf16[128,512]{1,0:T(8,128)(2,1)S(1)}, bf16[128,512]{1,0:T(8,128)(2,1)}, u32[]{:S(2)}) copy-start(bf16[128,512]{1,0:T(8,128)(2,1)} %get-tuple-element.13) | copy-start | bytes 393220
  111.2 3.1 %copy-start.1 = (bf16[128,512]{1,0:T(8,128)(2,1)S(1)}, bf16[128,512]{1,0:T(8,128)(2,1)}, u32[]{:S(2)}) copy-start(bf16[128,512]{1,0:T(8,128)(2,1)} %get-tuple-element.14) | copy-start | bytes 393220
  111.2 3.7 %copy-start.4 = (bf16[32,512]{1,0:T(8,128)(2,1)S(1)}, bf16[32,512]{1,0:T(8,128)(2,1)}, u32[]{:S(2)}) copy-start(bf16[32,512]{1,0:T(8,128)(2,1)} %get-tuple-element.15) | copy-start | bytes 98308
  111.2 4.3 %copy-start.3 = (bf16[32,512]{1,0:T(8,128)(2,1)S(1)}, bf16[32,512]{1,0:T(8,128)(2,1)}, u32[]{:S(2)}) copy-start(bf16[32,512]{1,0:T(8,128)(2,1)} %get-tuple-element.16) | copy-start | bytes 98308
  111.2 4.9 %copy-start = (bf16[256,512]{1,0:T(8,128)(2,1)S(1)}, bf16[256,512]{1,0:T(8,128)(2,1)}, u32[]{:S(2)}) copy-start(bf16[256,512]{1,0:T(8,128)(2,1)} %get-tuple-element.29) | copy-start | bytes 786436

commit v2 on v1

v2 whole, which is shorter than its diff:
```python
import jax
import jax.numpy as jnp
from jax import lax
from jax.experimental import pallas as pl
from jax.experimental.pallas import tpu as pltpu
from jax.sharding import PartitionSpec as P

MESH = pl.DeviceIdType.MESH
BF = jnp.bfloat16
F32 = jnp.float32
HD = 128
NY = 4
NJ = 4
NDP = 8
TOK = 128
OLDT = 32
ROWS = 1024
CHUNK = 512
SCALE = HD**-0.5
EXPC = SCALE * 1.4426950408889634
NEG = -1e30
SENDS, RECVS = 180, 220
UNITS = [(i, c) for i in range(4) for c in range(i + 2)]
UNIT = {u: n for n, u in enumerate(UNITS)}


def dot(a, b):
    return jnp.dot(a, b, preferred_element_type=F32)


def dot_nt(a, b):
    return lax.dot_general(a, b, (((1,), (1,)), ((), ())), preferred_element_type=F32)


def kernel(
    q_ref, k_ref, v_ref, ok_ref, ov_ref, g_ref, x_ref, reads_ref,
    dq_ref, dk_ref, dv_ref, odk_ref, odv_ref, dw_ref,
    xin, xloc, xall, qb, gb, kc, ko, kst, kt, ebuf, sbuf, linv, lcol, gl, ql, dqb,
    vacc, part, opart, m1, m2, m3, mrg, rold, vg4, og4, vgall,
    wp, wown, ry, wz, rz, wfin, ssem, rsem, lsem,
):
    seq = lax.axis_index("seq")
    p = lax.axis_index("pool")
    dp = lax.axis_index("dp")
    y = seq // NJ
    j = seq % NJ
    z = 2 * j + p
    x = dp // 2
    core = dp % 2
    jr = (j + 1) % NJ
    jl = (j + 3) % NJ
    jo = (j + 2) % NJ

    def at_y(yy):
        return (yy * NJ + j, p, dp)

    def at_j(jj, pp=None):
        return (y * NJ + jj, p if pp is None else pp, dp)

    def at_dp(dd):
        return (seq, p, dd)

    count = {"s": 0, "r": 0, "l": 0}
    sends = []

    def take(kind, n=1):
        base = count[kind]
        count[kind] += n
        return base

    def send(src, dst, rs, dev):
        c = pltpu.make_async_remote_copy(
            src_ref=src, dst_ref=dst, send_sem=ssem.at[take("s")], recv_sem=rsem.at[rs],
            device_id=dev, device_id_type=MESH,
        )
        c.start()
        sends.append(c)

    def arrived(dst, rs):
        pltpu.make_async_copy(dst, dst, rsem.at[rs]).wait()

    def local(src, dst):
        c = pltpu.make_async_copy(src, dst, lsem.at[take("l")])
        c.start()
        return c

    barrier = pltpu.get_barrier_semaphore()
    peers = [at_y((y + r) % NY) for r in range(1, NY)]
    peers += [at_j(((z + t) % 8) // 2, ((z + t) % 8) % 2) for t in range(1, 8)]
    peers += [at_dp((dp + t) % NDP) for t in range(1, NDP)]
    for dev in peers:
        pl.semaphore_signal(barrier, inc=1, device_id=dev, device_id_type=MESH)
    pl.semaphore_wait(barrier, len(peers))

    def col(n, width=HD):
        return pl.ds(pl.multiple_of(n * width, width), width)

    def lanes(hp):
        return pl.ds(hp * 256, 256)

    def quarter(n, hp):
        return pl.ds(pl.multiple_of(n * ROWS + hp * 256, 256), 256)

    r_kv = [[take("r") for _ in range(3)] for _ in range(2)]
    r_ov = [[take("r") for _ in range(3)] for _ in range(2)]
    r_q = [take("r", 4) for _ in range(4)]
    r_g = [take("r", 4) for _ in range(4)]
    loc_kv = []

    def send_kv(a, cur, old):
        for r in range(1, NY):
            yy = (y + r) % NY
            send(cur.at[:, col(yy)], kc.at[a, y, j], r_kv[a][r - 1], at_y(yy))
            send(old.at[:, col(yy)], kst.at[a, y], r_ov[a][r - 1], at_y(yy))
        loc_kv.append(
            (local(cur.at[:, col(y)], kc.at[a, y, j]), local(old.at[:, col(y)], kst.at[a, y]))
        )

    def send_rows(ref, buf, base, hp):
        for r in (2, 1, 3):
            yy = (y + r) % NY
            send(ref.at[:, quarter(yy, hp)], buf.at[y, :, lanes(hp)], base[hp] + r, at_y(yy))

    def rows_arrived(buf, base, hp):
        for r in range(1, NY):
            arrived(buf.at[(y + NY - r) % NY, :, lanes(hp)], base[hp] + r)

    send_kv(0, k_ref, ok_ref)
    send_rows(q_ref, qb, r_q, 0)
    loc_x = local(x_ref, xin)
    loc_q = local(q_ref.at[:, col(y, ROWS)], qb.at[y])
    loc_g = local(g_ref.at[:, col(y, ROWS)], gb.at[y])

    r_side = [[take("r", 2), take("r", 2)] for _ in range(2)]
    r_fwd = [[take("r"), take("r")] for _ in range(2)]
    r_oz = [take("r", 4) for _ in range(2)]

    def gather_start(a):
        loc_kv[a][0].wait()
        loc_kv[a][1].wait()
        for r in range(1, NY):
            yy = (y + NY - r) % NY
            arrived(kc.at[a, yy, j], r_kv[a][r - 1])
            arrived(kst.at[a, yy], r_ov[a][r - 1])
        low, high = kc.at[a, 0:2, j], kc.at[a, 2:4, j]
        send(low, low, r_side[a][0], at_j(jr))
        send(high, high, r_side[a][1], at_j(jl))
        send(high, high, r_side[a][0] + 1, at_j(jr))
        send(low, low, r_side[a][1] + 1, at_j(jl))

    def gather_forward(a):
        arrived(kc.at[a, 0:2, jl], r_side[a][0])
        send(kc.at[a, 0:2, jl], kc.at[a, 0:2, jl], r_fwd[a][0], at_j(jr))
        arrived(kc.at[a, 2:4, jr], r_side[a][1])
        send(kc.at[a, 2:4, jr], kc.at[a, 2:4, jr], r_fwd[a][1], at_j(jl))
        for t in range(NJ):
            jj = (j + t) % NJ
            send(kst.at[a], ko.at[a, :, j], r_oz[a] + t, at_j(jj, 1 - p))

    def gather_end(a):
        arrived(kc.at[a, 2:4, jl], r_side[a][0] + 1)
        arrived(kc.at[a, 0:2, jr], r_side[a][1] + 1)
        arrived(kc.at[a, 0:2, jo], r_fwd[a][0])
        arrived(kc.at[a, 2:4, jo], r_fwd[a][1])
        for t in range(NJ):
            arrived(ko.at[a, :, (j + NJ - t) % NJ], r_oz[a] + t)

    def chunk(a, c):
        if c == 0:
            return ko[a].reshape(CHUNK, HD)
        return kc[a, c - 1].reshape(CHUNK, HD)

    gather_start(0)
    for hp in range(1, 4):
        send_rows(q_ref, qb, r_q, hp)

    loc_x.wait()

    def turn(b, _):
        for half in range(2):
            block = xin[:, pl.ds(pl.multiple_of(b * 256 + half * 128, 128), 128)]
            xloc[b, pl.ds(half * 4, 4)] = block.T.reshape(4, 32, TOK)
        return 0

    lax.fori_loop(0, 32, turn, 0, unroll=4)
    r_x = take("r", 8)
    loc_xx = local(xloc.at[:, dp], xall.at[:, :, col(dp)])
    for t in range(1, NDP):
        dd = (dp + t) % NDP
        send(xloc.at[:, dd], xall.at[:, :, col(dp)], r_x + t, at_dp(dd))

    gather_forward(0)
    send_kv(1, v_ref, ov_ref)
    for hp in range(4):
        rows_arrived(qb, r_q, hp)
    for hp in range(4):
        send_rows(g_ref, gb, r_g, hp)
    loc_q.wait()
    gather_end(0)
    for c in range(5):
        kt[c] = chunk(0, c).T
    gather_start(1)

    def heads(ref, i, hp):
        block = ref[i, :, lanes(hp)]
        return jnp.concatenate([block[:, :HD], block[:, HD:]], axis=0)

    bias = [
        [(jnp.minimum(reads_ref[s, n], 1) - 1).astype(F32) * (-NEG) for n in range(4)]
        for s in range(2)
    ]

    def probs(hp, i):
        qh = heads(qb, i, hp)
        top = None
        slot = i % 2
        for c in range(i + 2):
            s = dot_nt(chunk(0, c), qh)
            if c == 0:
                s = jnp.concatenate(
                    [s[n * 128:(n + 1) * 128] + bias[i // 2][n] for n in range(4)], axis=0
                )
            elif c == i + 1:
                ahead = lax.broadcasted_iota(jnp.int32, s.shape, 0) - lax.broadcasted_iota(
                    jnp.int32, s.shape, 1
                ) % TOK
                s = jnp.where(ahead <= TOK * j, s, NEG)
            sbuf[slot, c] = s
            high = jnp.max(s, axis=0, keepdims=True)
            top = high if top is None else jnp.maximum(top, high)
        total = None
        for c in range(i + 2):
            e = jnp.exp2((sbuf[slot, c] - top) * EXPC)
            add = jnp.sum(e, axis=0, keepdims=True)
            total = add if total is None else total + add
            ebuf[UNIT[i, c], :, lanes(hp)] = e.astype(BF)
        linv[i, :, lanes(hp)] = 1.0 / total

    for hp in range(4):
        for i in range(4):
            probs(hp, i)
        if hp == 1:
            gather_forward(1)

    def spread(hp):
        for i in range(4):
            for h in (2 * hp, 2 * hp + 1):
                at = pl.ds(h * HD, HD)
                inv = jnp.broadcast_to(linv[i, :, at], (HD, HD)).T
                lcol[i, at, :] = inv
                gl[i, at, :] = (gb[i, :, at].astype(F32) * inv).astype(BF)

    def spread_q(n, _):
        i = n // 8
        h = n % 8
        at = pl.ds(pl.multiple_of(h * HD, HD), HD)
        ql[i, at, :] = (qb[i, :, at].astype(F32) * (lcol[i, at, :] * SCALE)).astype(BF)
        return 0

    def keys_grad(right, c, rows=slice(None)):
        acc = None
        for i in range(max(c - 1, 0), 4):
            term = dot(ebuf[UNIT[i, c], :, rows], right[i, rows])
            acc = term if acc is None else acc + term
        return acc

    def keep(a, c, acc):
        if c == 0:
            opart[a] = acc.astype(BF).reshape(NY, NJ, OLDT, HD)
        else:
            part[a, c - 1] = acc.astype(BF).reshape(NJ, TOK, HD)

    r_m1 = [[take("r"), take("r")] for _ in range(2)]
    r_m2 = [[take("r"), take("r")] for _ in range(2)]
    r_m3 = [[take("r"), take("r")] for _ in range(2)]
    r_old = [take("r", 4) for _ in range(2)]

    def sum_low(a):
        send(part.at[a, 0:2, jo], m1.at[a, 0], r_m1[a][0], at_j(jr))
        send(part.at[a, 0:2, jl], m2.at[a, 0], r_m2[a][1], at_j(jl))

    def sum_high(a):
        send(part.at[a, 2:4, jo], m1.at[a, 1], r_m1[a][1], at_j(jl))
        send(part.at[a, 2:4, jr], m2.at[a, 1], r_m2[a][0], at_j(jr))

    def sum_merge(a):
        arrived(m1.at[a, 0], r_m1[a][0])
        mrg[a, 0] = (m1[a, 0].astype(F32) + part[a, 0:2, jr].astype(F32)).astype(BF)
        send(mrg.at[a, 0], m3.at[a, 0], r_m3[a][0], at_j(jr))
        arrived(m1.at[a, 1], r_m1[a][1])
        mrg[a, 1] = (m1[a, 1].astype(F32) + part[a, 2:4, jl].astype(F32)).astype(BF)
        send(mrg.at[a, 1], m3.at[a, 1], r_m3[a][1], at_j(jl))
        for t in range(NJ):
            jj = (j + t) % NJ
            send(opart.at[a, :, jj], rold.at[a, t], r_old[a] + t, at_j(jj, 1 - p))

    r_fin = [take("r", 4) for _ in range(2)]
    r_ofin = [take("r", 4) for _ in range(2)]

    def sum_end(a, put):
        arrived(m2.at[a, 1], r_m2[a][0])
        arrived(m2.at[a, 0], r_m2[a][1])
        arrived(m3.at[a, 0], r_m3[a][0])
        arrived(m3.at[a, 1], r_m3[a][1])
        for half in range(2):
            vg4[a, pl.ds(half * 2, 2)] = (
                part[a, pl.ds(half * 2, 2), j].astype(F32)
                + m2[a, half].astype(F32)
                + m3[a, half].astype(F32)
            ).astype(BF)
        own = local(vg4.at[a, y], put)
        for r in range(1, NY):
            yy = (y + r) % NY
            send(vg4.at[a, yy], put, r_fin[a] + r, at_y(yy))
        return own

    def sum_old(a, oput):
        for t in range(NJ):
            arrived(rold.at[a, t], r_old[a] + t)
        og4[a] = (
            rold[a, 0].astype(F32) + rold[a, 1].astype(F32)
            + rold[a, 2].astype(F32) + rold[a, 3].astype(F32)
        ).astype(BF)
        oown_copy = local(og4.at[a, y], oput)
        for r in range(1, NY):
            yy = (y + r) % NY
            send(og4.at[a, yy], oput, r_ofin[a] + r, at_y(yy))
        return oown_copy

    def by_head(copy, base, whole):
        copy.wait()
        for r in range(1, NY):
            arrived(whole.at[:, col((y + NY - r) % NY)], base + r)

    loc_g.wait()
    first, second = pl.ds(0, 512), pl.ds(512, 512)
    for hp in range(2):
        rows_arrived(gb, r_g, hp)
        spread(hp)
    for c in range(5):
        vacc[c] = keys_grad(gl, c, first)
    for hp in range(2, 4):
        rows_arrived(gb, r_g, hp)
        spread(hp)
    for c in (1, 2, 3, 4, 0):
        keep(1, c, vacc[c] + keys_grad(gl, c, second))
        if c == 2:
            sum_low(1)
        if c == 4:
            sum_high(1)

    gather_end(1)
    r_dq = [take("r", 4) for _ in range(4)]

    def scores_grad(hp, i):
        gh = heads(gb, i, hp)
        inv = linv[i, :, lanes(hp)]
        slot = i % 2
        delta = None
        for c in range(i + 2):
            d = dot_nt(chunk(1, c), gh)
            sbuf[slot, c] = d
            add = jnp.sum(ebuf[UNIT[i, c], :, lanes(hp)].astype(F32) * d, axis=0, keepdims=True)
            delta = add if delta is None else delta + add
        delta = delta * inv
        acc = None
        for c in range(i + 2):
            t = (ebuf[UNIT[i, c], :, lanes(hp)].astype(F32) * (sbuf[slot, c] - delta)).astype(BF)
            ebuf[UNIT[i, c], :, lanes(hp)] = t
            term = dot(kt[c], t)
            acc = term if acc is None else acc + term
        acc = acc * (inv * SCALE)
        out = jnp.concatenate([acc[:, :HD].T, acc[:, HD:].T], axis=1)
        dqb[i, :, lanes(hp)] = out.astype(BF)

    loc_dq = []

    def send_dq(hp):
        loc_dq.append(local(dqb.at[y, :, lanes(hp)], dq_ref.at[:, quarter(y, hp)]))
        for r in range(1, NY):
            yy = (y + r) % NY
            send(dqb.at[yy, :, lanes(hp)], dq_ref.at[:, quarter(y, hp)], r_dq[hp] + r, at_y(yy))

    for i in range(4):
        scores_grad(0, i)
    send_dq(0)
    scores_grad(1, 0)
    sum_merge(1)
    for i in range(1, 4):
        scores_grad(1, i)
    send_dq(1)
    v_own = sum_end(1, vgall.at[dp, :, col(y)])
    for i in range(4):
        scores_grad(2, i)
    send_dq(2)
    r_vg = take("r", 4)
    r_vs = take("r", 4)
    by_head(v_own, r_fin[1], vgall.at[dp])
    sib = 2 * x + 1 - core
    for t in (1, 3, 2):
        send(vgall.at[dp], vgall.at[dp], r_vg + t, at_dp(2 * ((x + t) % 4) + core))
    send(vgall.at[dp], vgall.at[dp], r_vs, at_dp(sib))
    dv_copy = local(vgall.at[dp], dv_ref)
    for i in range(4):
        scores_grad(3, i)
    send_dq(3)
    ov_own = sum_old(1, odv_ref.at[:, col(y)])
    lax.fori_loop(0, 32, spread_q, 0, unroll=8)
    for c in (1, 2):
        keep(0, c, keys_grad(ql, c))
    sum_low(0)
    for t in (1, 3, 2):
        d = 2 * ((x + 4 - t) % 4) + core
        arrived(vgall.at[d], r_vg + t)
        send(vgall.at[d], vgall.at[d], r_vs + t, at_dp(sib))

    loc_xx.wait()
    for t in range(1, NDP):
        arrived(xall.at[:, :, col((dp + NDP - t) % NDP)], r_x + t)
    for c in (3, 4):
        keep(0, c, keys_grad(ql, c))
    sum_high(0)
    for t in range(4):
        arrived(vgall.at[2 * ((x + 4 - t) % 4) + 1 - core], r_vs + t)
    r_wy = [take("r", 4), take("r", 4)]

    def weight(yy):
        left = xall[pl.ds(yy * 8, 8)].reshape(256, NDP * TOK)
        return dot(left, vgall[...].reshape(NDP * TOK, 4 * HD)).reshape(8, 32, 4 * HD)

    for r in (2, 1, 3):
        yy = (y + r) % NY
        both = weight(yy).astype(BF)
        wp[r - 1, 0] = both[:, :16]
        wp[r - 1, 1] = both[:, 16:]
        send(wp.at[r - 1, 0], ry.at[r - 1, 0], r_wy[0] + r, at_y(yy))
    for r in (2, 1, 3):
        send(wp.at[r - 1, 1], ry.at[r - 1, 1], r_wy[1] + r, at_y((y + r) % NY))
    keep(0, 0, keys_grad(ql, 0))
    sum_merge(0)
    both = weight(y)
    wown[0] = both[:, :16]
    wown[1] = both[:, 16:]
    r_wz = [take("r", 8), take("r", 8)]
    r_wd = [take("r", 8), take("r", 8)]

    def weight_y(h):
        for r in range(1, NY):
            arrived(ry.at[r - 1, h], r_wy[h] + r)
        wz[h] = (
            wown[h] + ry[0, h].astype(F32) + ry[1, h].astype(F32) + ry[2, h].astype(F32)
        ).astype(BF)
        for t in (4, 3, 5, 2, 6, 1, 7):
            zz = (z + t) % 8
            send(wz.at[h, zz], rz.at[t - 1, h], r_wz[h] + t, at_j(zz // 2, zz % 2))

    def rows(d, h):
        return pl.ds(pl.multiple_of(d * 32 + h * 16, 16), 16)

    def weight_z(h):
        acc = wz[h, z].astype(F32)
        for t in range(1, 8):
            arrived(rz.at[t - 1, h], r_wz[h] + t)
            acc = acc + rz[t - 1, h].astype(F32)
        wfin[h] = (acc * (1.0 / 256.0)).astype(BF)
        own = local(wfin.at[h], dw_ref.at[rows(dp, h)])
        for t in (4, 3, 5, 2, 6, 1, 7):
            send(wfin.at[h], dw_ref.at[rows(dp, h)], r_wd[h] + t, at_dp((dp + t) % NDP))
        return own

    weight_y(0)
    k_own = sum_end(0, dk_ref.at[:, col(y)])
    weight_y(1)
    ok_own = sum_old(0, odk_ref.at[:, col(y)])
    own_w = [weight_z(0), weight_z(1)]

    by_head(k_own, r_fin[0], dk_ref)
    by_head(ok_own, r_ofin[0], odk_ref)
    by_head(ov_own, r_ofin[1], odv_ref)
    dv_copy.wait()
    for hp in range(4):
        loc_dq[hp].wait()
        for r in range(1, NY):
            arrived(dq_ref.at[:, quarter((y + NY - r) % NY, hp)], r_dq[hp] + r)
    for h in range(2):
        own_w[h].wait()
        for t in range(1, NDP):
            arrived(dw_ref.at[rows((dp + NDP - t) % NDP, h)], r_wd[h] + t)
    for c in sends:
        c.wait_send()
    assert count["s"] <= ssem.shape[0] and count["r"] <= rsem.shape[0]
    assert count["l"] <= lsem.shape[0]


def deliver(*refs):
    source, target, held = refs[:6], refs[6:12], refs[12:18]
    sem_in, sem_out = refs[18:]
    inward = [pltpu.make_async_copy(source[n], held[n], sem_in.at[n]) for n in range(6)]
    outward = [pltpu.make_async_copy(held[n], target[n], sem_out.at[n]) for n in range(6)]
    for c in inward:
        c.start()
    for n in range(6):
        inward[n].wait()
        outward[n].start()
    for c in outward:
        c.wait()


def on_device(queries, keys, values, old_keys, old_values, out_grad, inputs, reads):
    anywhere = pl.BlockSpec(memory_space=pl.ANY)
    out = [(TOK, 4096), (TOK, 512), (TOK, 512), (OLDT, 512), (OLDT, 512), (256, 512)]
    bf = lambda *shape: pltpu.VMEM(shape, BF)
    f32 = lambda *shape: pltpu.VMEM(shape, F32)
    results = pl.pallas_call(
        kernel,
        out_shape=[jax.ShapeDtypeStruct(shape, BF) for shape in out],
        in_specs=[anywhere] * 7 + [pl.BlockSpec(memory_space=pltpu.SMEM)],
        out_specs=[anywhere] * 6,
        scratch_shapes=[
            bf(TOK, 8192),
            bf(32, 8, 32, TOK),
            bf(32, 32, NDP * TOK),
            bf(4, TOK, ROWS),
            bf(4, TOK, ROWS),
            bf(2, NY, NJ, TOK, HD),
            bf(2, NY, NJ, OLDT, HD),
            bf(2, NY, OLDT, HD),
            bf(5, HD, CHUNK),
            bf(len(UNITS), CHUNK, ROWS),
            f32(2, 5, CHUNK, 256),
            f32(4, 1, ROWS),
            f32(4, ROWS, HD),
            bf(4, ROWS, HD),
            bf(4, ROWS, HD),
            bf(4, TOK, ROWS),
            f32(5, CHUNK, HD),
            bf(2, NY, NJ, TOK, HD),
            bf(2, NY, NJ, OLDT, HD),
            bf(2, 2, 2, TOK, HD),
            bf(2, 2, 2, TOK, HD),
            bf(2, 2, 2, TOK, HD),
            bf(2, 2, 2, TOK, HD),
            bf(2, NJ, NY, OLDT, HD),
            bf(2, NY, TOK, HD),
            bf(2, NY, OLDT, HD),
            bf(NDP, TOK, 512),
            bf(3, 2, 8, 16, 512),
            f32(2, 8, 16, 512),
            bf(3, 2, 8, 16, 512),
            bf(2, 8, 16, 512),
            bf(7, 2, 16, 512),
            bf(2, 16, 512),
            pltpu.SemaphoreType.DMA((SENDS,)),
            pltpu.SemaphoreType.DMA((RECVS,)),
            pltpu.SemaphoreType.DMA((24,)),
        ],
        compiler_params=pltpu.CompilerParams(
            collective_id=0, has_side_effects=True, vmem_limit_bytes=56 * 1024 * 1024
        ),
        cost_estimate=pl.CostEstimate(
            flops=11_000_000_000, bytes_accessed=10_000_000, transcendentals=8_000_000
        ),
    )(
        queries[0, 0], keys[0, 0], values[0, 0], old_keys[0, 0], old_values[0, 0],
        out_grad[0, 0], inputs[0, 0], reads[0, 0],
    )
    results = pl.pallas_call(
        deliver,
        out_shape=[jax.ShapeDtypeStruct(shape, BF) for shape in out],
        in_specs=[anywhere] * 6,
        out_specs=[anywhere] * 6,
        scratch_shapes=[bf(*shape) for shape in out]
        + [pltpu.SemaphoreType.DMA((6,)), pltpu.SemaphoreType.DMA((6,))],
    )(*results)
    return tuple(r[None, None] for r in results[:5]) + (results[5],)


def solution(mesh):
    token = P("dp", "pool", "seq", None)
    in_specs = (token,) * 7 + (P("dp", "pool", None, None),)
    out_specs = (token,) * 5 + (P(("seq", "pool"), None),)
    return jax.shard_map(
        on_device, mesh=mesh, in_specs=in_specs, out_specs=out_specs, check_vma=False
    )
```

time: 117 us -> 101 us (0.86)
  Pallas kernels: 109 us -> 99.9 us
  local copies, waits for them, and re-layouts: 5.62 us -> 0 us
  other arithmetic: 1.25 us -> 0 us
    pallas_call x1, Pallas kernels: 109 us -> 97.4 us  [on_device(): pl.pallas_call(kernel, out_shape=[jax.ShapeDtypeStruct(shape, BF) for sha...]
    unnamed x16 -> x0, local copies, waits for them, and re-layouts: 5.62 us -> none
    pallas_call x0 -> x1, Pallas kernels: none -> 2.49 us  [on_device(): pl.pallas_call(deliver, out_shape=[jax.ShapeDtypeStruct(shape, BF) for sh...]
    mul x1 -> x0, other arithmetic: 1.25 us -> none  [on_device(): bias = (jnp.minimum(reads[0, 0], 1).astype(F32) - 1.0) * -NEG]
where the time goes in v2:
time: 101 us
  Pallas kernels  99.9 us (99%)
    pallas_call x1, Pallas kernels, on_device(): pl.pallas_call(kernel, out_shape=[jax.ShapeDtypeStruct(shape, BF) for sha...  97.4 us
    pallas_call x1, Pallas kernels, on_device(): pl.pallas_call(deliver, out_shape=[jax.ShapeDtypeStruct(shape, BF) for sh...  2.49 us

profile of v2, /device:TPU:1, one launch (start us, length us, event | category | flops | bytes accessed | tf_op | source)
XLA Modules:
  0.0 100.7 jit_solution(10912382918291544461)
XLA Ops:
  0.6 97.4 %shard_map.127 = (bf16[128,4096]{1,0:T(8,128)(2,1)}, bf16[128,512]{1,0:T(8,128)(2,1)}, bf16[128,512]{1,0:T(8,128)(2,1)}, bf16[32,512]{1,0:T(8,128)(2,1)}, bf16[3...) custom-call(bf16[128,4096]{1,0:T(8,128)(2,1)} %bitcast.14, bf16[128,512]{1,0:T(8,128)(2,1)} %bitcast.17, ...), custom_call_target="tpu_custom_call" | custom-call | flops 11000000512 | bytes 10000000 | tf_op jit(solution)/shard_map/pallas_call | solution.py:514
  98.1 2.5 %shard_map.128 = (bf16[128,4096]{1,0:T(8,128)(2,1)}, bf16[128,512]{1,0:T(8,128)(2,1)}, bf16[128,512]{1,0:T(8,128)(2,1)}, bf16[32,512]{1,0:T(8,128)(2,1)}, bf16[3...) custom-call(bf16[128,4096]{1,0:T(8,128)(2,1)} %get-tuple-element.18.refs_0_, bf16[128,512]{1,0:T(8,128)(2,1)} %get-tuple-element.19.refs_1_, ...), custom_call_target="tpu_custom_call" | custom-call | tf_op jit(solution)/shard_map/pallas_call | solution.py:567

commit v3 on v2

--- a/solution.py
+++ b/solution.py
@@ -101,6 +101,9 @@
     def quarter(n, hp):
         return pl.ds(pl.multiple_of(n * ROWS + hp * 256, 256), 256)
 
+    def half_of(n, hp):
+        return pl.ds(pl.multiple_of(n * ROWS + hp * 256, 512), 512)
+
     r_kv = [[take("r") for _ in range(3)] for _ in range(2)]
     r_ov = [[take("r") for _ in range(3)] for _ in range(2)]
     r_q = [take("r", 4) for _ in range(4)]
@@ -174,6 +177,9 @@
     for hp in range(1, 4):
         send_rows(q_ref, qb, r_q, hp)
 
+    gather_forward(0)
+    send_kv(1, v_ref, ov_ref)
+
     loc_x.wait()
 
     def turn(b, _):
@@ -189,8 +195,6 @@
         dd = (dp + t) % NDP
         send(xloc.at[:, dd], xall.at[:, :, col(dp)], r_x + t, at_dp(dd))
 
-    gather_forward(0)
-    send_kv(1, v_ref, ov_ref)
     for hp in range(4):
         rows_arrived(qb, r_q, hp)
     for hp in range(4):
@@ -376,23 +380,25 @@
     loc_dq = []
 
     def send_dq(hp):
-        loc_dq.append(local(dqb.at[y, :, lanes(hp)], dq_ref.at[:, quarter(y, hp)]))
+        at = pl.ds(hp * 256, 512)
+        loc_dq.append(local(dqb.at[y, :, at], dq_ref.at[:, half_of(y, hp)]))
         for r in range(1, NY):
             yy = (y + r) % NY
-            send(dqb.at[yy, :, lanes(hp)], dq_ref.at[:, quarter(y, hp)], r_dq[hp] + r, at_y(yy))
+            send(dqb.at[yy, :, at], dq_ref.at[:, half_of(y, hp)], r_dq[hp] + r, at_y(yy))
 
     for i in range(4):
         scores_grad(0, i)
+    lax.fori_loop(0, 32, spread_q, 0, unroll=8)
+    scores_grad(1, 0)
+    scores_grad(1, 1)
+    sum_merge(1)
+    scores_grad(1, 2)
+    scores_grad(1, 3)
     send_dq(0)
-    scores_grad(1, 0)
-    sum_merge(1)
+    scores_grad(2, 0)
+    v_own = sum_end(1, vgall.at[dp, :, col(y)])
     for i in range(1, 4):
-        scores_grad(1, i)
-    send_dq(1)
-    v_own = sum_end(1, vgall.at[dp, :, col(y)])
-    for i in range(4):
         scores_grad(2, i)
-    send_dq(2)
     r_vg = take("r", 4)
     r_vs = take("r", 4)
     by_head(v_own, r_fin[1], vgall.at[dp])
@@ -403,9 +409,7 @@
     dv_copy = local(vgall.at[dp], dv_ref)
     for i in range(4):
         scores_grad(3, i)
-    send_dq(3)
-    ov_own = sum_old(1, odv_ref.at[:, col(y)])
-    lax.fori_loop(0, 32, spread_q, 0, unroll=8)
+    send_dq(2)
     for c in (1, 2):
         keep(0, c, keys_grad(ql, c))
     sum_low(0)
@@ -417,9 +421,6 @@
     loc_xx.wait()
     for t in range(1, NDP):
         arrived(xall.at[:, :, col((dp + NDP - t) % NDP)], r_x + t)
-    for c in (3, 4):
-        keep(0, c, keys_grad(ql, c))
-    sum_high(0)
     for t in range(4):
         arrived(vgall.at[2 * ((x + 4 - t) % 4) + 1 - core], r_vs + t)
     r_wy = [take("r", 4), take("r", 4)]
@@ -436,7 +437,11 @@
         send(wp.at[r - 1, 0], ry.at[r - 1, 0], r_wy[0] + r, at_y(yy))
     for r in (2, 1, 3):
         send(wp.at[r - 1, 1], ry.at[r - 1, 1], r_wy[1] + r, at_y((y + r) % NY))
+    for c in (3, 4):
+        keep(0, c, keys_grad(ql, c))
+    sum_high(0)
     keep(0, 0, keys_grad(ql, 0))
+    ov_own = sum_old(1, odv_ref.at[:, col(y)])
     sum_merge(0)
     both = weight(y)
     wown[0] = both[:, :16]
@@ -468,25 +473,28 @@
             send(wfin.at[h], dw_ref.at[rows(dp, h)], r_wd[h] + t, at_dp((dp + t) % NDP))
         return own
 
+    early = len(sends)
     weight_y(0)
     k_own = sum_end(0, dk_ref.at[:, col(y)])
     weight_y(1)
     ok_own = sum_old(0, odk_ref.at[:, col(y)])
+    by_head(ov_own, r_ofin[1], odv_ref)
+    dv_copy.wait()
+    for hp in (0, 2):
+        loc_dq[hp // 2].wait()
+        for r in range(1, NY):
+            arrived(dq_ref.at[:, half_of((y + NY - r) % NY, hp)], r_dq[hp] + r)
+    for c in sends[:early]:
+        c.wait_send()
     own_w = [weight_z(0), weight_z(1)]
 
     by_head(k_own, r_fin[0], dk_ref)
     by_head(ok_own, r_ofin[0], odk_ref)
-    by_head(ov_own, r_ofin[1], odv_ref)
-    dv_copy.wait()
-    for hp in range(4):
-        loc_dq[hp].wait()
-        for r in range(1, NY):
-            arrived(dq_ref.at[:, quarter((y + NY - r) % NY, hp)], r_dq[hp] + r)
     for h in range(2):
         own_w[h].wait()
         for t in range(1, NDP):
             arrived(dw_ref.at[rows((dp + NDP - t) % NDP, h)], r_wd[h] + t)
-    for c in sends:
+    for c in sends[early:]:
         c.wait_send()
     assert count["s"] <= ssem.shape[0] and count["r"] <= rsem.shape[0]
     assert count["l"] <= lsem.shape[0]

time: 101 us -> 98.5 us (0.975)
  Pallas kernels: 99.9 us -> 97.6 us
    pallas_call x1, Pallas kernels: 97.4 us -> 95.1 us  [on_device(): pl.pallas_call(kernel, out_shape=[jax.ShapeDtypeStruct(shape, BF) for sha...]
where the time goes in v3:
time: 98.5 us; the launch traced here: 98.4 us
  Pallas kernels  97.6 us (99%)
    pallas_call x1, Pallas kernels, on_device(): pl.pallas_call(kernel, out_shape=[jax.ShapeDtypeStruct(shape, BF) for sha...  95.1 us
    pallas_call x1, Pallas kernels, on_device(): pl.pallas_call(deliver, out_shape=[jax.ShapeDtypeStruct(shape, BF) for sh...  2.49 us

profile of v3, /device:TPU:1, one launch (start us, length us, event | category | flops | bytes accessed | tf_op | source)
XLA Modules:
  0.0 98.4 jit_solution(9721281656476349707)
XLA Ops:
  0.6 95.1 %shard_map.127 = (bf16[128,4096]{1,0:T(8,128)(2,1)}, bf16[128,512]{1,0:T(8,128)(2,1)}, bf16[128,512]{1,0:T(8,128)(2,1)}, bf16[32,512]{1,0:T(8,128)(2,1)}, bf16[3...) custom-call(bf16[128,4096]{1,0:T(8,128)(2,1)} %bitcast.14, bf16[128,512]{1,0:T(8,128)(2,1)} %bitcast.17, ...), custom_call_target="tpu_custom_call" | custom-call | flops 11000000512 | bytes 10000000 | tf_op jit(solution)/shard_map/pallas_call | solution.py:522
  95.7 2.5 %shard_map.128 = (bf16[128,4096]{1,0:T(8,128)(2,1)}, bf16[128,512]{1,0:T(8,128)(2,1)}, bf16[128,512]{1,0:T(8,128)(2,1)}, bf16[32,512]{1,0:T(8,128)(2,1)}, bf16[3...) custom-call(bf16[128,4096]{1,0:T(8,128)(2,1)} %get-tuple-element.18.refs_0_, bf16[128,512]{1,0:T(8,128)(2,1)} %get-tuple-element.19.refs_1_, ...), custom_call_target="tpu_custom_call" | custom-call | tf_op jit(solution)/shard_map/pallas_call | solution.py:575
